TPU v7x, 32 devices: a whole 2x2x4 slice. The times are simulated.
32 devices in a mesh: groups: 2 (over y), seq: 4 (over z), dp: 2 (over x), strand: 2 (over core).
Axes of the slice: x: 2, y: 2, z: 4, core: 2. Of those that a mesh axis runs over, the one named last changes fastest.
Arguments:
- tokens: int32 [4, 2048], P(('groups', 'dp'), 'seq'), parts along dimension 0, may hold values from 0 to 3
- stem_table: bfloat16 [15, 4, 1536], replicated, may hold values from -1.5 to 1.5
- conv_weight: bfloat16 [3, 1536, 768], P(None, 'dp'), may hold values from -0.09375 to 0.09375
- gain_in: float32 [1536], replicated, may hold values from 0.1 to 1.9
- gain_mid: float32 [768], replicated, may hold values from 0.1 to 1.9
- point_weight: bfloat16 [768, 1536], P('dp'), may hold values from -0.21875 to 0.21875
Outputs:
- embedding: bfloat16 [4, 2048, 1536], P(('groups', 'dp'), 'seq', 'strand'), parts along dimension 0
There are 2 independent parts, one for each index of `groups`. A program takes and returns all parts, laid end to end along the dimension named above; an argument that names none is the same for every part. Nothing has to cross between parts.
All inputs are finite; a program needn't handle non-finite values.
Results may differ from a plain program's by a relative error of at most 0.009.
Values may be sent and summed in bfloat16 or wider, within the bound.
No kernel may reach another device: no remote copies, remote signals or barrier semaphores. Data moves between devices by JAX's collectives and lax.ppermute only.
A program may use at most 64 MiB of HBM per device.

v0:
```python
import jax
import jax.numpy as jnp
from jax import lax
from jax.sharding import PartitionSpec as P

DILATION_STEP = 256


def swapped(value, axis, distance):
    mask = 2**distance
    pairs = [(source, source ^ mask) for source in range(lax.axis_size(axis))]
    return lax.ppermute(value, axis, pairs)


def padded(block, sides, width):
    for axis, dim in sides:
        count = lax.axis_size(axis)
        forward = [(i, i + 1) for i in range(count - 1)]
        backward = [(target, source) for source, target in forward]
        low = lax.ppermute(
            lax.slice_in_dim(block, block.shape[dim] - width, None, axis=dim), axis, forward
        )
        high = lax.ppermute(lax.slice_in_dim(block, 0, width, axis=dim), axis, backward)
        block = jnp.concatenate([low, block, high], axis=dim)
    return block


def normalize(values, gain):
    scale = lax.rsqrt(jnp.mean(values * values, axis=-1, keepdims=True) + 1e-06)
    return jax.nn.gelu(values * scale * gain)


def per_device(tokens, stem_table, conv_weight, gain_in, gain_mid, point_weight):
    row_count = tokens.shape[1]
    width = stem_table.shape[2]
    inner = conv_weight.shape[2]
    tap_total = stem_table.shape[0]
    kinds = stem_table.shape[1]
    strand = lax.axis_index("strand")
    second = strand == 1
    base_ids = tokens[0]
    bit_count = lax.axis_size("seq").bit_length() - 1
    flipped = base_ids
    for bit_index in range(bit_count):
        flipped = swapped(flipped, "seq", bit_index)
    used_ids = jnp.where(second, 3 - flipped[::-1], base_ids)
    flipped_tap = jnp.zeros((), jnp.bool_)
    rim_width = tap_total // 2
    shifted = padded(used_ids + 1, (("seq", 0),), rim_width) - 1
    onehot = (shifted[:, None] == jnp.arange(kinds, dtype=jnp.int32)[None, :]).astype(jnp.bfloat16)
    windows = jnp.concatenate(
        [onehot[tap_position : tap_position + row_count] for tap_position in range(tap_total)],
        axis=1,
    )
    embedded = jnp.dot(
        windows, stem_table.reshape(tap_total * kinds, width), preferred_element_type=jnp.float32
    ).astype(jnp.bfloat16)
    stream = embedded.astype(jnp.float32)
    gelu_output = normalize(stream, gain_in).astype(jnp.bfloat16)
    padded_activation = padded(gelu_output, (("seq", 0),), DILATION_STEP)
    tap_offsets = [
        jnp.where(
            flipped_tap, (2 - tap_position) * DILATION_STEP, tap_position * DILATION_STEP
        ).astype(jnp.int32)
        for tap_position in range(3)
    ]
    carry_sum = jnp.zeros((row_count, inner), jnp.float32)
    weight_block = lax.all_gather(conv_weight, "dp", axis=1, tiled=True)
    block_rows = weight_block.shape[1]
    for tap_position in range(3):
        tap_slices = lax.dynamic_slice(
            padded_activation, (tap_offsets[tap_position], 0), (row_count, block_rows)
        )
        carry_sum = carry_sum + jnp.dot(
            tap_slices, weight_block[tap_position], preferred_element_type=jnp.float32
        )
    middle = normalize(carry_sum, gain_mid).astype(jnp.bfloat16)
    tap_slices = middle
    branch = jnp.dot(
        tap_slices,
        lax.all_gather(point_weight, "dp", axis=0, tiled=True),
        preferred_element_type=jnp.float32,
    )
    layer_out = (stream + branch).astype(jnp.bfloat16)
    returned = layer_out
    for bit_index in range(bit_count):
        returned = swapped(returned, "seq", bit_index)
    strand_term = jnp.where(second, returned[::-1], layer_out)
    half_width = width // 2
    kept_half = lax.dynamic_slice_in_dim(strand_term, strand * half_width, half_width, 1)
    sent_half = lax.dynamic_slice_in_dim(strand_term, (1 - strand) * half_width, half_width, 1)
    received = swapped(sent_half, "strand", 0)
    summed = kept_half.astype(jnp.float32) + received.astype(jnp.float32)
    return (summed * 0.5).astype(jnp.bfloat16)[None]


def solution(mesh):
    return jax.shard_map(
        per_device,
        mesh=mesh,
        in_specs=(P(("groups", "dp"), "seq"), P(), P(None, "dp", None), P(), P(), P("dp", None)),
        out_specs=P(("groups", "dp"), "seq", "strand"),
        check_vma=False,
    )
```

profile of v0, /device:TPU:0, one launch (start us, length us, event | category | flops | bytes accessed | tf_op | source)
XLA Modules:
  0.0 263.3 jit_solution(4680295752803171987)
XLA Ops:
  7.3 3.1 %collective-permute-start = (s32[512]{0:T(512)S(1)}, s32[512]{0:T(512)S(1)}, u32[]{:S(2)}, u32[]{:S(2)}) collective-permute-start(s32[512]{0:T(512)S(1)} %bitcast.20), channel_id=1, source_target_pairs={{0,4},{4,0},{8,12},{12,8},{1,5},{5,1},{9,13},{13,9},{2,6},{6,2},{1... | collective-permute-start | bytes 6152 | tf_op jit(solution)/shard_map/ppermute | solution.py:12
  10.4 1.6 collective-permute-done
  12.0 3.0 %collective-permute-start.1 = (s32[512]{0:T(512)S(1)}, s32[512]{0:T(512)S(1)}, u32[]{:S(2)}, u32[]{:S(2)}) collective-permute-start(s32[512]{0:T(512)S(1)} %collective-permute-done), channel_id=1, source_target_pairs={{0,8},{4,12},{8,0},{12,4},{1,9},{5,13},{9,1},{13,5},{2,10},{6,14},... | collective-permute-start | bytes 6152 | tf_op jit(solution)/shard_map/ppermute | solution.py:12
  15.1 1.5 collective-permute-done.1
  16.7 3.8 %collective-permute-start.2 = (s32[7]{0:T(128)S(1)}, s32[7]{0:T(128)S(1)}, u32[]{:S(2)}, u32[]{:S(2)}) collective-permute-start(s32[7]{0:T(128)S(1)} %get-tuple-element.22), channel_id=1, source_target_pairs={{0,4},{4,8},{8,12},{1,5},{5,9},{9,13},{2,6},{6,10},{10,14},{3,7},{... | collective-permute-start | bytes 92 | tf_op jit(solution)/shard_map/ppermute | solution.py:20
  20.6 1.3 collective-permute-start.3
  21.9 4.1 %collective-permute-done.3 = s32[7]{0:T(128)S(1)} collective-permute-done((s32[7]{0:T(128)S(1)}, s32[7]{0:T(128)S(1)}, u32[]{:S(2)}, u32[]{:S(2)}) %collective-permute-start.3) | collective-permute-done | bytes 60 | tf_op jit(solution)/shard_map/ppermute | solution.py:23
  28.1 1.4 fusion.4
  30.4 4.4 %collective-permute-start.4 = (bf16[256,1536]{1,0:T(8,128)(2,1)S(1)}, bf16[256,1536]{1,0:T(8,128)(2,1)}, u32[]{:S(2)}, u32[]{:S(2)}) collective-permute-start(bf16[256,1536]{1,0:T(8,128)(2,1)S(1)} %get-tuple-element.6), channel_id=1, source_target_pairs={{0,4},{4,8},{8,12},{1,5},{5,9},{9,13},{2,6},{6,10},{10,14},{3,7},{... | collective-permute-start | bytes 2359304 | tf_op jit(solution)/shard_map/ppermute | solution.py:20
  34.8 1.3 collective-permute-start.5
  36.1 10.9 %collective-permute-done.4 = bf16[256,1536]{1,0:T(8,128)(2,1)} collective-permute-done((bf16[256,1536]{1,0:T(8,128)(2,1)S(1)}, bf16[256,1536]{1,0:T(8,128)(2,1)}, u32[]{:S(2)}, u32[]{:S(2)}) %collective-permute-start.4) | collective-permute-done | bytes 786464 | tf_op jit(solution)/shard_map/ppermute | solution.py:20
  47.0 53.9 %all-gather.3.cloned.1.call-done = bf16[3,1536,768]{2,1,0:T(8,128)(2,1)} async-done(((bf16[3,768,768]{2,1,0:T(8,128)(2,1)}), bf16[3,1536,768]{2,1,0:T(8,128)(2,1)}) %all-gather.3.cloned.1.call-update) | async-done | bytes 7077904 | tf_op jit(solution)/shard_map/all_gather | solution.py:68
  100.9 3.4 %fusion.13 = f32[512,768]{1,0:T(8,128)S(1)} fusion(bf16[3,1536,768]{2,1,0:T(8,128)(2,1)} %all-gather.3.cloned.1.call-done, bf16[512,1536]{1,0:T(8,128)(2,1)S(1)} %fusion.4, bf16[256,1536]{1,0:T(8,128)(2,1)} %collective-permute-done.4), kind=kOutput, calls=%fused_computation.22 | convolution fusion | flops 1211105280 | bytes 6291456 | tf_op jit(solution)/shard_map/dot_general | solution.py:74
  104.8 1.4 fusion.12
  106.2 3.7 %multiply_reduce_fusion = (f32[512]{0:T(512)S(1)}, f32[512,768]{1,0:T(8,128)}) fusion(bf16[3,1536,768]{2,1,0:T(8,128)(2,1)S(1)} %copy-done.4, bf16[256,1536]{1,0:T(8,128)(2,1)} %collective-permute-done.5, bf16[512,1536]{1,0:T(8,128)(2,1)S(1)} %fusion.4, f32[512,768]{1,0:T(8,128)S(1)} %fusion.13, f32[512,768]{1,0:T(8,128)S(1)} %fusion.12), kind=kOutput, calls=%fused_computation.36 | convolution fusion | flops 1212677632 | bytes 9439232 | tf_op jit(solution)/shard_map/dot_general | solution.py:74
  110.0 28.5 %all-gather.5.cloned.1.call-done = bf16[768,1536]{1,0:T(8,128)(2,1)} async-done(((bf16[384,1536]{1,0:T(8,128)(2,1)}), bf16[768,1536]{1,0:T(8,128)(2,1)}) %all-gather.5.cloned.1.call-update) | async-done | bytes 2359312 | tf_op jit(solution)/shard_map/all_gather | solution.py:81
  138.5 3.8 %fusion.10 = bf16[512,1536]{1,0:T(8,128)(2,1)S(1)} fusion(bf16[768,1536]{1,0:T(8,128)(2,1)} %all-gather.5.cloned.1.call-done, bf16[512,1536]{1,0:T(8,128)(2,1)S(1)} %get-tuple-element.25, f32[512,768]{1,0:T(8,128)} %get-tuple-element.27, f32[768]{0:T(1024)S(1)} %copy-done.5, f32[512]{0:T(512)S(1)} %add_rsqrt_fusion), kind=kOutput, calls=%fused_computation.14 | convolution fusion | flops 1214644224 | bytes 7083008 | tf_op jit(solution)/shard_map/dot_general | solution.py:79
  143.5 1.5 collective-permute-start.6
  145.0 34.6 %collective-permute-done.6 = bf16[512,1536]{1,0:T(8,128)(2,1)S(1)} collective-permute-done((bf16[512,1536]{1,0:T(8,128)(2,1)S(1)}, bf16[512,1536]{1,0:T(8,128)(2,1)S(1)}, u32[]{:S(2)}, u32[]{:S(2)}) %collective-permute-start.6) | collective-permute-done | bytes 1572896 | tf_op jit(solution)/shard_map/ppermute | solution.py:12
  179.7 2.4 collective-permute-start.7
  182.1 67.4 %collective-permute-done.7 = bf16[512,1536]{1,0:T(8,128)(2,1)S(1)} collective-permute-done((bf16[512,1536]{1,0:T(8,128)(2,1)S(1)}, bf16[512,1536]{1,0:T(8,128)(2,1)S(1)}, u32[]{:S(2)}, u32[]{:S(2)}) %collective-permute-start.7) | collective-permute-done | bytes 1572896 | tf_op jit(solution)/shard_map/ppermute | solution.py:12
  249.5 1.8 rev.7
  251.3 1.6 broadcast_select_fusion
  253.1 2.3 collective-permute-done.8
  (33 shorter events, 7.0 us)
Async XLA Ops:
  6.5 0.8 copy-start.3
  6.5 8.5 %copy-start.1 = (bf16[15,4,1536]{2,1,0:T(4,128)(2,1)S(1)}, bf16[15,4,1536]{2,1,0:T(4,128)(2,1)}, u32[]{:S(2)}) copy-start(bf16[15,4,1536]{2,1,0:T(4,128)(2,1)} %param.7) | copy-start | bytes 552964
  6.5 94.3 %all-gather.3.cloned.1.call-start = ((), (), s32[]{:S(2)}) async-start(), calls=%async_computation | async-start | bytes 10616832 | tf_op jit(solution)/shard_map/all_gather | solution.py:68
  7.3 131.3 %all-gather.5.cloned.1.call-start = ((), (), s32[]{:S(2)}) async-start(), calls=%async_computation.1 | async-start | bytes 3538944 | tf_op jit(solution)/shard_map/all_gather | solution.py:81
  7.3 4.7 %collective-permute-start = (s32[512]{0:T(512)S(1)}, s32[512]{0:T(512)S(1)}, u32[]{:S(2)}, u32[]{:S(2)}) collective-permute-start(s32[512]{0:T(512)S(1)} %bitcast.20), channel_id=1, source_target_pairs={{0,4},{4,0},{8,12},{12,8},{1,5},{5,1},{9,13},{13,9},{2,6},{6,2},{1... | collective-permute-start | bytes 6152 | tf_op jit(solution)/shard_map/ppermute | solution.py:12
  12.0 4.6 %collective-permute-start.1 = (s32[512]{0:T(512)S(1)}, s32[512]{0:T(512)S(1)}, u32[]{:S(2)}, u32[]{:S(2)}) collective-permute-start(s32[512]{0:T(512)S(1)} %collective-permute-done), channel_id=1, source_target_pairs={{0,8},{4,12},{8,0},{12,4},{1,9},{5,13},{9,1},{13,5},{2,10},{6,14},... | collective-permute-start | bytes 6152 | tf_op jit(solution)/shard_map/ppermute | solution.py:12
  16.7 5.1 %collective-permute-start.2 = (s32[7]{0:T(128)S(1)}, s32[7]{0:T(128)S(1)}, u32[]{:S(2)}, u32[]{:S(2)}) collective-permute-start(s32[7]{0:T(128)S(1)} %get-tuple-element.22), channel_id=1, source_target_pairs={{0,4},{4,8},{8,12},{1,5},{5,9},{9,13},{2,6},{6,10},{10,14},{3,7},{... | collective-permute-start | bytes 92 | tf_op jit(solution)/shard_map/ppermute | solution.py:20
  20.6 5.4 %collective-permute-start.3 = (s32[7]{0:T(128)S(1)}, s32[7]{0:T(128)S(1)}, u32[]{:S(2)}, u32[]{:S(2)}) collective-permute-start(s32[7]{0:T(128)S(1)} %get-tuple-element.23), channel_id=1, source_target_pairs={{4,0},{8,4},{12,8},{5,1},{9,5},{13,9},{6,2},{10,6},{14,10},{7,3},{... | collective-permute-start | bytes 92 | tf_op jit(solution)/shard_map/ppermute | solution.py:23
  26.6 1.5 copy-start.2
  30.4 16.5 %collective-permute-start.4 = (bf16[256,1536]{1,0:T(8,128)(2,1)S(1)}, bf16[256,1536]{1,0:T(8,128)(2,1)}, u32[]{:S(2)}, u32[]{:S(2)}) collective-permute-start(bf16[256,1536]{1,0:T(8,128)(2,1)S(1)} %get-tuple-element.6), channel_id=1, source_target_pairs={{0,4},{4,8},{8,12},{1,5},{5,9},{9,13},{2,6},{6,10},{10,14},{3,7},{... | collective-permute-start | bytes 2359304 | tf_op jit(solution)/shard_map/ppermute | solution.py:20
  34.8 71.4 %collective-permute-start.5 = (bf16[256,1536]{1,0:T(8,128)(2,1)}, bf16[256,1536]{1,0:T(8,128)(2,1)}, u32[]{:S(2)}, u32[]{:S(2)}) collective-permute-start(bf16[256,1536]{1,0:T(8,128)(2,1)} %get-tuple-element.5), channel_id=1, source_target_pairs={{4,0},{8,4},{12,8},{5,1},{9,5},{13,9},{6,2},{10,6},{14,10},{7,3},{... | collective-permute-start | bytes 2359304 | tf_op jit(solution)/shard_map/ppermute | solution.py:23
  100.9 4.0 %copy-start.4 = (bf16[3,1536,768]{2,1,0:T(8,128)(2,1)S(1)}, bf16[3,1536,768]{2,1,0:T(8,128)(2,1)}, u32[]{:S(2)}) copy-start(bf16[3,1536,768]{2,1,0:T(8,128)(2,1)} %all-gather.3.cloned.1.call-done) | copy-start | bytes 21233668
  106.2 32.3 %copy-start.5 = (f32[768]{0:T(1024)S(1)}, f32[768]{0:T(1024)}, u32[]{:S(2)}) copy-start(f32[768]{0:T(1024)} %param.10) | copy-start | bytes 9220
  142.3 1.2 copy-start
  143.5 36.1 %collective-permute-start.6 = (bf16[512,1536]{1,0:T(8,128)(2,1)S(1)}, bf16[512,1536]{1,0:T(8,128)(2,1)S(1)}, u32[]{:S(2)}, u32[]{:S(2)}) collective-permute-start(bf16[512,1536]{1,0:T(8,128)(2,1)S(1)} %fusion.10), channel_id=1, source_target_pairs={{0,4},{4,0},{8,12},{12,8},{1,5},{5,1},{9,13},{13,9},{2,6},{6,2},{1... | collective-permute-start | bytes 4718600 | tf_op jit(solution)/shard_map/ppermute | solution.py:12
  179.7 69.9 %collective-permute-start.7 = (bf16[512,1536]{1,0:T(8,128)(2,1)S(1)}, bf16[512,1536]{1,0:T(8,128)(2,1)S(1)}, u32[]{:S(2)}, u32[]{:S(2)}) collective-permute-start(bf16[512,1536]{1,0:T(8,128)(2,1)S(1)} %collective-permute-done.6), channel_id=1, source_target_pairs={{0,8},{4,12},{8,0},{12,4},{1,9},{5,13},{9,1},{13,5},{2,10},{6,14},... | collective-permute-start | bytes 4718600 | tf_op jit(solution)/shard_map/ppermute | solution.py:12
  253.0 2.4 collective-permute-start.8
Sparse Core Ops, SparseCore 0:
  8.9 91.9 all-gather.2
  102.4 36.0 all-gather.4
where the time goes:
time: 264 us; the launch traced here: 263 us
  waiting for transfers between devices  206 us (78%)
  starting transfers between devices  20.9 us (8%)
  between operations  13.6 us (5%)
  matrix products  13 us (5%)
  local copies, waits for them, and re-layouts  5.97 us (2%)
  other arithmetic  4.3 us (2%)
    ppermute x5, waiting for transfers between devices, swapped(): return lax.ppermute(value, axis, pairs)  107 us
    all_gather x1, waiting for transfers between devices, per_device(): weight_block = lax.all_gather(conv_weight, 'dp', axis=1, tiled=True)  53.9 us
    all_gather x1, waiting for transfers between devices, per_device(): lax.all_gather(point_weight, 'dp', axis=0, tiled=True)  28.5 us
    ppermute x2, waiting for transfers between devices, padded(): lax.ppermute(lax.slice_in_dim(block, block.shape[dim] - width, None, axis...  10.9 us
    ppermute x5, starting transfers between devices, swapped(): return lax.ppermute(value, axis, pairs)  10.1 us
    dot_general x3, matrix products, per_device(): jnp.dot(tap_slices, weight_block[tap_position], preferred_element_type=jn...  8.55 us
    ppermute x2, starting transfers between devices, padded(): lax.ppermute(lax.slice_in_dim(block, block.shape[dim] - width, None, axis...  8.17 us
  transfers between devices with their start and end apart: 11, of which 9 were waited for; matrix products, arithmetic and copies ran while one was open for 5% of the time, Pallas kernels for 0%

commit v1 on v0

v1 whole, which is shorter than its diff:
```python
import functools

import jax
import jax.numpy as jnp
from jax import lax
from jax.experimental import pallas as pl
from jax.experimental.pallas import tpu as pltpu
from jax.sharding import PartitionSpec as P

DILATION = 256
REACH = 384
EPS = 1e-06
ROW_STEP = 128
VMEM_BYTES = 24 * 2**20


def shifted_pairs(axis, distance):
    count = lax.axis_size(axis)
    return [(i, i + distance) for i in range(count) if 0 <= i + distance < count]


def ring_pairs(axis, distance):
    count = lax.axis_size(axis)
    return [(i, (i + distance) % count) for i in range(count)]


def one_hot_columns(tok_ref, row_count, length):
    span = row_count + 2 * DILATION
    width = tok_ref.shape[1]
    spread = jnp.broadcast_to(tok_ref[...], (16, width))
    start = width - (REACH - DILATION + 8)
    taps = pltpu.roll(spread, start, 1, stride=1, stride_axis=0)[:, :span]
    lane = lax.broadcasted_iota(jnp.int32, (16, span), 1)
    place = lane + (lax.axis_index("seq") * row_count - DILATION)
    source = place + 8 - lax.broadcasted_iota(jnp.int32, (16, span), 0)
    inside = (place >= 0) & (place < length) & (source >= 0) & (source < length)
    taps = jnp.where(inside, taps, -1)
    hot = jnp.concatenate([(taps == base).astype(jnp.float32) for base in range(4)], axis=0)
    return hot.T.astype(jnp.bfloat16)


def gelu(x):
    inner = x * (0.7978845608028654 + 0.035677408136300125 * (x * x))
    half = 0.5 * x
    return half + half * jnp.tanh(inner)


def partial_kernel(own, length, *refs):
    if own:
        tok_ref, table_ref, both_ref, gain_ref, w_any, out_ref, res_ref, w_ref, act_ref, sem = refs
    else:
        tok_ref, table_ref, gain_ref, w_any, out_ref, w_ref, act_ref, sem = refs
    row_count = out_ref.shape[0]
    depth = gain_ref.shape[1]
    copy = pltpu.make_async_copy(w_any, w_ref, sem)
    copy.start()
    hot = one_hot_columns(tok_ref, row_count, length)
    if own:
        here = hot[DILATION : DILATION + row_count]
        twice = jnp.concatenate([here, here], axis=1)
        res_ref[...] = jnp.dot(twice, both_ref[...], preferred_element_type=jnp.float32)
    gain = gain_ref[...]
    for low in range(0, row_count + 2 * DILATION, ROW_STEP):
        embedded = jnp.dot(
            hot[low : low + ROW_STEP], table_ref[...], preferred_element_type=jnp.float32
        )
        mean = jnp.mean(embedded * embedded, axis=-1, keepdims=True)
        scaled = embedded[:, :depth] * lax.rsqrt(mean + EPS) * gain
        act_ref[low : low + ROW_STEP] = gelu(scaled).astype(jnp.bfloat16)
    copy.wait()
    second = lax.axis_index("strand")
    for low in range(0, row_count, DILATION):
        total = None
        for tap in range(3):
            weight = w_ref[tap + second * (2 - 2 * tap)]
            start = low + tap * DILATION
            part = jnp.dot(
                act_ref[start : start + DILATION], weight, preferred_element_type=jnp.float32
            )
            total = part if total is None else total + part
        out_ref[low : low + DILATION] = total.astype(out_ref.dtype)


def partial_call(own, length, row_count, operands):
    depth, inner = operands[-1].shape[1:]
    vmem = pl.BlockSpec(memory_space=pltpu.VMEM)
    outs = [jax.ShapeDtypeStruct((row_count, inner), jnp.float32 if own else jnp.bfloat16)]
    if own:
        outs.append(jax.ShapeDtypeStruct((row_count, operands[2].shape[1]), jnp.float32))
    return pl.pallas_call(
        functools.partial(partial_kernel, own, length),
        out_shape=outs,
        in_specs=[vmem] * (len(operands) - 1) + [pl.BlockSpec(memory_space=pl.ANY)],
        out_specs=[vmem] * len(outs),
        scratch_shapes=[
            pltpu.VMEM(operands[-1].shape, jnp.bfloat16),
            pltpu.VMEM((row_count + 2 * DILATION, depth), jnp.bfloat16),
            pltpu.SemaphoreType.DMA,
        ],
        compiler_params=pltpu.CompilerParams(vmem_limit_bytes=VMEM_BYTES),
        cost_estimate=pl.CostEstimate(
            flops=6 * row_count * depth * inner, bytes_accessed=12 * 2**20, transcendentals=0
        ),
        name="conv_own" if own else "conv_sent",
    )(*operands)


def middle_kernel(count, *refs):
    own_ref, gain_ref, out_ref = refs[0], refs[count], refs[count + 1]
    for low in range(0, own_ref.shape[0], ROW_STEP):
        rows = slice(low, low + ROW_STEP)
        total = own_ref[rows]
        for ref in refs[1:count]:
            total = total + ref[rows].astype(jnp.float32)
        mean = jnp.mean(total * total, axis=-1, keepdims=True)
        out_ref[rows] = gelu(total * lax.rsqrt(mean + EPS) * gain_ref[...]).astype(jnp.bfloat16)


def final_kernel(count, *refs):
    mine_ref, other_ref, res_ref = refs[:3]
    blocks = refs[3 : 3 + count]
    out_ref, weight_ref, sems = refs[3 + count :]
    depth = blocks[0].shape[0]
    me = lax.axis_index("dp")
    copies = []
    for step, block in enumerate(blocks):
        place = pl.multiple_of(lax.rem(me + step, count) * depth, 16)
        copy = pltpu.make_async_copy(block, weight_ref.at[pl.ds(place, depth)], sems.at[step])
        copy.start()
        copies.append(copy)
    total = mine_ref[...].astype(jnp.float32) + other_ref[...].astype(jnp.float32)
    total = total.astype(jnp.bfloat16)
    for copy in copies:
        copy.wait()
    branch = jnp.dot(total, weight_ref[...], preferred_element_type=jnp.float32)
    out_ref[...] = (0.5 * (branch + res_ref[...])).astype(jnp.bfloat16)


def per_device(tokens, stem_table, conv_weight, gain_in, gain_mid, point_weight):
    row_count = tokens.shape[1]
    tap_total, kinds, width = stem_table.shape
    depth, inner = conv_weight.shape[1:]
    count = lax.axis_size("dp")
    length = row_count * lax.axis_size("seq")
    me = lax.axis_index("dp")
    strand = lax.axis_index("strand")
    second = strand == 1
    half = width // 2
    vmem = pl.BlockSpec(memory_space=pltpu.VMEM)
    params = pltpu.CompilerParams(vmem_limit_bytes=VMEM_BYTES)

    base_ids = tokens[0]
    low = lax.ppermute(base_ids[row_count - REACH :], "seq", shifted_pairs("seq", 1))
    high = lax.ppermute(base_ids[:REACH], "seq", shifted_pairs("seq", -1))
    near = jnp.concatenate([low, base_ids, high])[None]
    sequences = [near] + [
        lax.ppermute(near, "dp", ring_pairs("dp", -step)) for step in range(1, count)
    ]

    by_base = jnp.swapaxes(stem_table, 0, 1)
    blank = jnp.zeros((kinds, 1, width), stem_table.dtype)
    straight = jnp.concatenate([blank, by_base[:, ::-1]], axis=1).reshape(kinds * 16, width)
    flipped = jnp.concatenate([blank, by_base[::-1]], axis=1).reshape(kinds * 16, width)
    table = jnp.where(second, flipped, straight)
    table = lax.dynamic_slice_in_dim(
        jnp.concatenate([table, table], axis=1), me * depth, width, axis=1
    )
    both = lax.dynamic_slice_in_dim(
        jnp.concatenate([straight, flipped], axis=0), strand * half, half, axis=1
    )
    gain_here = lax.dynamic_slice_in_dim(gain_in, me * depth, depth)[None]

    columns = lax.dynamic_slice_in_dim(point_weight, strand * half, half, axis=1)
    blocks = [columns] + [
        lax.ppermute(columns, "dp", ring_pairs("dp", -step)) for step in range(1, count)
    ]

    received = []
    for step in range(1, count):
        (part,) = partial_call(
            False, length, row_count, (sequences[step], table, gain_here, conv_weight)
        )
        received.append(lax.ppermute(part, "dp", ring_pairs("dp", step)))
    own, res = partial_call(
        True, length, row_count, (near, table, both, gain_here, conv_weight)
    )
    middle = pl.pallas_call(
        functools.partial(middle_kernel, count),
        out_shape=jax.ShapeDtypeStruct((row_count, inner), jnp.bfloat16),
        in_specs=[vmem] * (count + 1),
        out_specs=vmem,
        compiler_params=params,
        name="middle",
    )(own, *received, gain_mid[None])
    other = lax.ppermute(middle, "strand", ring_pairs("strand", 1))
    out = pl.pallas_call(
        functools.partial(final_kernel, count),
        out_shape=jax.ShapeDtypeStruct((row_count, half), jnp.bfloat16),
        in_specs=[vmem] * 3 + [pl.BlockSpec(memory_space=pl.ANY)] * count,
        out_specs=vmem,
        scratch_shapes=[
            pltpu.VMEM((inner, half), jnp.bfloat16),
            pltpu.SemaphoreType.DMA((count,)),
        ],
        compiler_params=params,
        name="final",
    )(middle, other, res, *blocks)
    return out[None]


def solution(mesh):
    return jax.shard_map(
        per_device,
        mesh=mesh,
        in_specs=(P(("groups", "dp"), "seq"), P(), P(None, "dp", None), P(), P(), P("dp", None)),
        out_specs=P(("groups", "dp"), "seq", "strand"),
        check_vma=False,
    )
```

time: 264 us -> 60.9 us (0.23)
  waiting for transfers between devices: 206 us -> 25.3 us
  between operations: 13.6 us -> 0.2 us
  matrix products: 13 us -> 0 us
  Pallas kernels: 0 us -> 12.9 us
  starting transfers between devices: 20.9 us -> 11 us
  local copies, waits for them, and re-layouts: 5.97 us -> 10.8 us
  other arithmetic: 4.3 us -> 0.16 us
    ppermute x9 -> x6, waiting for transfers between devices: 122 us -> 25.3 us  [the longest x1 14.2 us: per_device(): lax.ppermute(columns, 'dp', ring_pairs('dp', -step))]
    all_gather x2 -> x0, waiting for transfers between devices: 82.4 us -> none  [the longest x1 53.9 us: per_device(): weight_block = lax.all_gather(conv_weight, 'dp', axis=1, tiled=True)]
    dot_general x5 -> x0, matrix products: 13 us -> none  [the longest x3 8.55 us: per_device(): jnp.dot(tap_slices, weight_block[tap_position], preferred_element_type=jn...]
    pallas_call x0 -> x4, Pallas kernels: none -> 12.9 us  [the longest x2 9.78 us: partial_call(): pl.pallas_call(functools.partial(partial_kernel, own, length), out_shape=...]
    ppermute x9 -> x6, starting transfers between devices: 20.8 us -> 11 us  [the longest x1 4.93 us: per_device(): lax.ppermute(base_ids[row_count - REACH:], 'seq', shifted_pairs('seq', 1))]
    rev x2, local copies, waits for them, and re-layouts: 1.92 us -> 5.63 us  [the longest x1 4.64 us: per_device(): by_base[::-1]]
  transfers between devices with their start and end apart: 11 -> 6, of which waited for: 9 -> 3; matrix products, arithmetic and copies ran while one was open for 5% -> 10% of each run, Pallas kernels for 0% -> 9%
where the time goes in v1:
time: 60.9 us; the launch traced here: 60.3 us
  waiting for transfers between devices  25.3 us (42%)
  Pallas kernels  12.9 us (21%)
  starting transfers between devices  11 us (18%)
  local copies, waits for them, and re-layouts  10.8 us (18%)
    ppermute x1, waiting for transfers between devices, per_device(): lax.ppermute(columns, 'dp', ring_pairs('dp', -step))  14.2 us
    pallas_call x2, Pallas kernels, partial_call(): pl.pallas_call(functools.partial(partial_kernel, own, length), out_shape=...  9.78 us
    ppermute x1, waiting for transfers between devices, per_device(): received.append(lax.ppermute(part, 'dp', ring_pairs('dp', step)))  9.15 us
    ppermute x1, starting transfers between devices, per_device(): lax.ppermute(base_ids[row_count - REACH:], 'seq', shifted_pairs('seq', 1))  4.93 us
    rev x1, local copies, waits for them, and re-layouts, per_device(): by_base[::-1]  4.64 us
    unnamed x14, local copies, waits for them, and re-layouts  4.09 us
    pallas_call x1, Pallas kernels, per_device(): pl.pallas_call(functools.partial(final_kernel, count), out_shape=jax.Shap...  2.32 us
    ppermute x1, waiting for transfers between devices, per_device(): lax.ppermute(near, 'dp', ring_pairs('dp', -step))  1.93 us
  transfers between devices with their start and end apart: 6, of which 3 were waited for; matrix products, arithmetic and copies ran while one was open for 10% of the time, Pallas kernels for 9%

profile of v1, /device:TPU:0, one launch (start us, length us, event | category | flops | bytes accessed | tf_op | source)
XLA Modules:
  0.0 60.3 jit_solution(13088789719374443284)
XLA Ops:
  0.0 0.8 %slice_reduce_fusion.1 = (s32[384]{0:T(512)S(1)}, s32[384]{0:T(512)S(1)}) fusion(s32[1,512]{1,0:T(1,128)} %param.6), kind=kLoop, calls=%fused_computation.9 | loop fusion | bytes 6144 | tf_op jit(solution)/shard_map/slice | solution.py:153
  0.8 4.9 %collective-permute-start = (s32[384]{0:T(512)S(1)}, s32[384]{0:T(512)S(1)}, u32[]{:S(2)}, u32[]{:S(2)}) collective-permute-start(s32[384]{0:T(512)S(1)} %get-tuple-element.9), channel_id=1, source_target_pairs={{0,4},{4,8},{8,12},{1,5},{5,9},{9,13},{2,6},{6,10},{10,14},{3,7},{... | collective-permute-start | bytes 4616 | tf_op jit(solution)/shard_map/ppermute | solution.py:153
  5.8 1.3 %collective-permute-start.1 = (s32[384]{0:T(512)S(1)}, s32[384]{0:T(512)S(1)}, u32[]{:S(2)}, u32[]{:S(2)}) collective-permute-start(s32[384]{0:T(512)S(1)} %get-tuple-element.10), channel_id=1, source_target_pairs={{4,0},{8,4},{12,8},{5,1},{9,5},{13,9},{6,2},{10,6},{14,10},{7,3},{... | collective-permute-start | bytes 4616 | tf_op jit(solution)/shard_map/ppermute | solution.py:154
  7.1 0.0 copy-start.5
  7.1 4.6 %rev.6 = bf16[4,15,1536]{2,0,1:T(4,128)(2,1)S(1)} reverse(bf16[4,15,1536]{2,0,1:T(4,128)(2,1)} %bitcast.9), dimensions={0} | reverse | bytes 368640 | tf_op jit(solution)/shard_map/rev | solution.py:163
  11.7 1.0 %rev.7 = bf16[4,15,1536]{2,0,1:T(4,128)(2,1)S(1)} reverse(bf16[4,15,1536]{2,0,1:T(4,128)(2,1)} %bitcast.10), dimensions={1} | reverse | bytes 368640 | tf_op jit(solution)/shard_map/rev | solution.py:162
  12.8 0.1 concatenate.16.clone
  12.9 0.1 concatenate.17.clone
  12.9 0.1 broadcast_select_fusion
  13.1 1.6 %collective-permute-start.2 = (s32[1,1280]{1,0:T(1,128)S(1)}, s32[1,1280]{1,0:T(1,128)S(1)}, u32[]{:S(2)}, u32[]{:S(2)}) collective-permute-start(s32[1,1280]{1,0:T(1,128)S(1)} %broadcast_in_dim.13.refs_0_), channel_id=1, source_target_pairs={{0,2},{2,0},{1,3},{3,1},{4,6},{6,4},{5,7},{7,5},{8,10},{10,8},{9,1... | collective-permute-start | bytes 15368 | tf_op jit(solution)/shard_map/ppermute | solution.py:157
  14.6 0.1 fusion.1.refs_1_
  14.7 0.1 dynamic_slice.14
  14.8 1.9 %collective-permute-done.2.refs_0_ = s32[1,1280]{1,0:T(1,128)S(1)} collective-permute-done((s32[1,1280]{1,0:T(1,128)S(1)}, s32[1,1280]{1,0:T(1,128)S(1)}, u32[]{:S(2)}, u32[]{:S(2)}) %collective-permute-start.2) | collective-permute-done | bytes 5152 | tf_op jit(solution)/shard_map/ppermute | solution.py:157
  16.7 2.0 %copy-done.1 = bf16[3,768,768]{2,1,0:T(8,128)(2,1)S(1)} copy-done((bf16[3,768,768]{2,1,0:T(8,128)(2,1)S(1)}, bf16[3,768,768]{2,1,0:T(8,128)(2,1)}, u32[]{:S(2)}) %copy-start.1) | copy-done | bytes 3538968
  18.7 4.6 %conv_sent.1 = bf16[512,768]{1,0:T(8,128)(2,1)S(1)} custom-call(s32[1,1280]{1,0:T(1,128)S(1)} %collective-permute-done.2.refs_0_, bf16[64,1536]{1,0:T(8,128)(2,1)S(1)} %fusion.1.refs_1_, f32[1,768]{1,0:T(1,128)S(1)} %broadcast_in_dim.14.refs_3_.refs_2_, bf16[3,768,768]{2,1,0:T(8,128)(2,1)S(1)} %copy-done.1), custom_call_target="tpu_custom_call" | custom-call | flops 1811939328 | bytes 12582912 | tf_op jit(solution)/shard_map/conv_sent/pallas_call | solution.py:90
  23.4 1.6 %collective-permute-start.3 = (bf16[512,768]{1,0:T(8,128)(2,1)S(1)}, bf16[512,768]{1,0:T(8,128)(2,1)S(1)}, u32[]{:S(2)}, u32[]{:S(2)}) collective-permute-start(bf16[512,768]{1,0:T(8,128)(2,1)S(1)} %conv_sent.1), channel_id=1, source_target_pairs={{0,2},{2,0},{1,3},{3,1},{4,6},{6,4},{5,7},{7,5},{8,10},{10,8},{9,1... | collective-permute-start | bytes 2359304 | tf_op jit(solution)/shard_map/ppermute | solution.py:183
  25.0 2.0 %copy-done.2 = bf16[3,768,768]{2,1,0:T(8,128)(2,1)S(1)} copy-done((bf16[3,768,768]{2,1,0:T(8,128)(2,1)S(1)}, bf16[3,768,768]{2,1,0:T(8,128)(2,1)}, u32[]{:S(2)}) %copy-start.2) | copy-done | bytes 3538968
  26.9 5.2 %conv_own.1 = (f32[512,768]{1,0:T(8,128)S(1)}, f32[512,768]{1,0:T(8,128)S(1)}) custom-call(s32[1,1280]{1,0:T(1,128)S(1)} %broadcast_in_dim.13.refs_0_, bf16[64,1536]{1,0:T(8,128)(2,1)S(1)} %fusion.1.refs_1_, bf16[128,768]{1,0:T(8,128)(2,1)S(1)} %fusion.refs_2_, f32[1,768]{1,0:T(1,128)S(1)} %broadcast_in_dim.14.refs_3_.refs_2_, bf16[3,768,768]{2,1,0:T(8,128)(2,1)S(1)} %copy-done.2), custom_call_target="tpu_custom_call" | custom-call | flops 1811939328 | bytes 12582912 | tf_op jit(solution)/shard_map/conv_own/pallas_call | solution.py:90
  32.1 9.1 %collective-permute-done.3.refs_1_ = bf16[512,768]{1,0:T(8,128)(2,1)S(1)} collective-permute-done((bf16[512,768]{1,0:T(8,128)(2,1)S(1)}, bf16[512,768]{1,0:T(8,128)(2,1)S(1)}, u32[]{:S(2)}, u32[]{:S(2)}) %collective-permute-start.3) | collective-permute-done | bytes 786464 | tf_op jit(solution)/shard_map/ppermute | solution.py:183
  41.3 0.8 %middle.1.refs_0_ = bf16[512,768]{1,0:T(8,128)(2,1)S(1)} custom-call(f32[512,768]{1,0:T(8,128)S(1)} %get-tuple-element.7.refs_0_, bf16[512,768]{1,0:T(8,128)(2,1)S(1)} %collective-permute-done.3.refs_1_, f32[1,768]{1,0:T(1,128)S(1)} %broadcast_in_dim.15.refs_2_), custom_call_target="tpu_custom_call" | custom-call | tf_op jit(solution)/shard_map/middle/pallas_call | solution.py:187
  42.1 0.1 collective-permute-start.4
  42.2 1.6 %collective-permute-start.5 = (bf16[384,768]{1,0:T(8,128)(2,1)S(1)}, bf16[384,768]{1,0:T(8,128)(2,1)S(1)}, u32[]{:S(2)}, u32[]{:S(2)}) collective-permute-start(bf16[384,768]{1,0:T(8,128)(2,1)S(1)} %constant_dynamic-slice_fusion.refs_3_), channel_id=1, source_target_pairs={{0,2},{2,0},{1,3},{3,1},{4,6},{6,4},{5,7},{7,5},{8,10},{10,8},{9,1... | collective-permute-start | bytes 1769480 | tf_op jit(solution)/shard_map/ppermute | solution.py:175
  43.8 14.2 %collective-permute-done.5.refs_4_ = bf16[384,768]{1,0:T(8,128)(2,1)S(1)} collective-permute-done((bf16[384,768]{1,0:T(8,128)(2,1)S(1)}, bf16[384,768]{1,0:T(8,128)(2,1)S(1)}, u32[]{:S(2)}, u32[]{:S(2)}) %collective-permute-start.5) | collective-permute-done | bytes 589856 | tf_op jit(solution)/shard_map/ppermute | solution.py:175
  58.0 2.3 %final.1 = bf16[512,768]{1,0:T(8,128)(2,1)} custom-call(bf16[512,768]{1,0:T(8,128)(2,1)S(1)} %middle.1.refs_0_, bf16[512,768]{1,0:T(8,128)(2,1)S(1)} %collective-permute-done.4.refs_1_, f32[512,768]{1,0:T(8,128)S(1)} %get-tuple-element.8.refs_2_, bf16[384,768]{1,0:T(8,128)(2,1)S(1)} %constant_dynamic-slice_fusion.refs_3_, ...), custom_call_target="tpu_custom_call" | custom-call | tf_op jit(solution)/shard_map/final/pallas_call | solution.py:196
  (20 shorter events, 0.2 us)
Async XLA Ops:
  0.0 42.2 %copy-start = (bf16[384,1536]{1,0:T(8,128)(2,1)S(1)}, bf16[384,1536]{1,0:T(8,128)(2,1)}, u32[]{:S(2)}) copy-start(bf16[384,1536]{1,0:T(8,128)(2,1)} %param.11) | copy-start | bytes 3538948
  0.0 13.0 %copy-start.3 = (s32[1,512]{1,0:T(1,128)S(1)}, s32[1,512]{1,0:T(1,128)}, u32[]{:S(2)}) copy-start(s32[1,512]{1,0:T(1,128)} %param.6) | copy-start | bytes 6148
  0.8 12.2 %collective-permute-start = (s32[384]{0:T(512)S(1)}, s32[384]{0:T(512)S(1)}, u32[]{:S(2)}, u32[]{:S(2)}) collective-permute-start(s32[384]{0:T(512)S(1)} %get-tuple-element.9), channel_id=1, source_target_pairs={{0,4},{4,8},{8,12},{1,5},{5,9},{9,13},{2,6},{6,10},{10,14},{3,7},{... | collective-permute-start | bytes 4616 | tf_op jit(solution)/shard_map/ppermute | solution.py:153
  5.8 7.3 %collective-permute-start.1 = (s32[384]{0:T(512)S(1)}, s32[384]{0:T(512)S(1)}, u32[]{:S(2)}, u32[]{:S(2)}) collective-permute-start(s32[384]{0:T(512)S(1)} %get-tuple-element.10), channel_id=1, source_target_pairs={{4,0},{8,4},{12,8},{5,1},{9,5},{13,9},{6,2},{10,6},{14,10},{7,3},{... | collective-permute-start | bytes 4616 | tf_op jit(solution)/shard_map/ppermute | solution.py:154
  7.1 7.6 %copy-start.5 = (f32[1536]{0:T(1024)S(1)}, f32[1536]{0:T(1024)}, u32[]{:S(2)}) copy-start(f32[1536]{0:T(1024)} %param.9) | copy-start | bytes 18436
  13.1 3.7 %collective-permute-start.2 = (s32[1,1280]{1,0:T(1,128)S(1)}, s32[1,1280]{1,0:T(1,128)S(1)}, u32[]{:S(2)}, u32[]{:S(2)}) collective-permute-start(s32[1,1280]{1,0:T(1,128)S(1)} %broadcast_in_dim.13.refs_0_), channel_id=1, source_target_pairs={{0,2},{2,0},{1,3},{3,1},{4,6},{6,4},{5,7},{7,5},{8,10},{10,8},{9,1... | collective-permute-start | bytes 15368 | tf_op jit(solution)/shard_map/ppermute | solution.py:157
  16.7 2.0 %copy-start.1 = (bf16[3,768,768]{2,1,0:T(8,128)(2,1)S(1)}, bf16[3,768,768]{2,1,0:T(8,128)(2,1)}, u32[]{:S(2)}) copy-start(bf16[3,768,768]{2,1,0:T(8,128)(2,1)} %refs_3_.1) | copy-start | bytes 10616836
  18.7 6.2 %copy-start.4 = (f32[768]{0:T(1024)S(1)}, f32[768]{0:T(1024)}, u32[]{:S(2)}) copy-start(f32[768]{0:T(1024)} %param.10) | copy-start | bytes 9220
  23.4 17.9 %collective-permute-start.3 = (bf16[512,768]{1,0:T(8,128)(2,1)S(1)}, bf16[512,768]{1,0:T(8,128)(2,1)S(1)}, u32[]{:S(2)}, u32[]{:S(2)}) collective-permute-start(bf16[512,768]{1,0:T(8,128)(2,1)S(1)} %conv_sent.1), channel_id=1, source_target_pairs={{0,2},{2,0},{1,3},{3,1},{4,6},{6,4},{5,7},{7,5},{8,10},{10,8},{9,1... | collective-permute-start | bytes 2359304 | tf_op jit(solution)/shard_map/ppermute | solution.py:183
  24.9 2.0 %copy-start.2 = (bf16[3,768,768]{2,1,0:T(8,128)(2,1)S(1)}, bf16[3,768,768]{2,1,0:T(8,128)(2,1)}, u32[]{:S(2)}) copy-start(bf16[3,768,768]{2,1,0:T(8,128)(2,1)} %refs_3_.1) | copy-start | bytes 10616836
  42.1 15.9 %collective-permute-start.4 = (bf16[512,768]{1,0:T(8,128)(2,1)S(1)}, bf16[512,768]{1,0:T(8,128)(2,1)S(1)}, u32[]{:S(2)}, u32[]{:S(2)}) collective-permute-start(bf16[512,768]{1,0:T(8,128)(2,1)S(1)} %middle.1.refs_0_), channel_id=1, source_target_pairs={{0,1},{1,0},{2,3},{3,2},{4,5},{5,4},{6,7},{7,6},{8,9},{9,8},{10,11... | collective-permute-start | bytes 2359304 | tf_op jit(solution)/shard_map/ppermute | solution.py:195
  42.2 15.8 %collective-permute-start.5 = (bf16[384,768]{1,0:T(8,128)(2,1)S(1)}, bf16[384,768]{1,0:T(8,128)(2,1)S(1)}, u32[]{:S(2)}, u32[]{:S(2)}) collective-permute-start(bf16[384,768]{1,0:T(8,128)(2,1)S(1)} %constant_dynamic-slice_fusion.refs_3_), channel_id=1, source_target_pairs={{0,2},{2,0},{1,3},{3,1},{4,6},{6,4},{5,7},{7,5},{8,10},{10,8},{9,1... | collective-permute-start | bytes 1769480 | tf_op jit(solution)/shard_map/ppermute | solution.py:175

commit v2 on v0

v2 whole, which is shorter than its diff:
```python
import functools

import jax
import jax.numpy as jnp
from jax import lax
from jax.experimental import pallas as pl
from jax.experimental.pallas import tpu as pltpu
from jax.sharding import PartitionSpec as P

DILATION = 256
REACH = 384
EPS = 1e-06
ROW_STEP = 128
KINDS = 4
MIB = 2**20


def shifted_pairs(axis, distance):
    count = lax.axis_size(axis)
    return [(i, i + distance) for i in range(count) if 0 <= i + distance < count]


def ring_pairs(axis, distance):
    count = lax.axis_size(axis)
    return [(i, (i + distance) % count) for i in range(count)]


def base_taps(tok_ref, row_count, length, low, span):
    width = tok_ref.shape[1]
    spread = jnp.broadcast_to(tok_ref[...], (16, width))
    start = width - (REACH - DILATION + low + 8)
    taps = pltpu.roll(spread, start, 1, stride=1, stride_axis=0)[:, :span]
    place = lax.broadcasted_iota(jnp.int32, (16, span), 1)
    place = place + (lax.axis_index("seq") * row_count - DILATION + low)
    source = place + 8 - lax.broadcasted_iota(jnp.int32, (16, span), 0)
    inside = (place >= 0) & (place < length) & (source >= 0) & (source < length)
    return jnp.where(inside, taps, -1).astype(jnp.float32).astype(jnp.bfloat16)


def one_hot(taps, second, table_rows):
    row = lax.broadcasted_iota(jnp.int32, (table_rows, 16), 0) // KINDS
    column = lax.broadcasted_iota(jnp.int32, (table_rows, 16), 1)
    chosen = (column == 15 - row + second * (2 * row - 14)).astype(jnp.float32)
    values = jnp.dot(chosen.astype(jnp.bfloat16), taps, preferred_element_type=jnp.float32)
    base = lax.broadcasted_iota(jnp.int32, values.shape, 0) % KINDS
    base = base + second * (KINDS - 1 - 2 * base)
    return (values == base.astype(jnp.float32)).astype(jnp.float32).T


def gelu(x):
    inner = x * (0.7978845608028654 + 0.035677408136300125 * (x * x))
    half = 0.5 * x
    return half + half * jnp.tanh(inner)


def activate(hot, table_ref, gain_ref, act_ref, low):
    depth = gain_ref.shape[1]
    for start in range(0, hot.shape[0], ROW_STEP):
        embedded = jnp.dot(
            hot[start : start + ROW_STEP], table_ref[...], preferred_element_type=jnp.float32
        )
        mean = jnp.mean(embedded * embedded, axis=-1, keepdims=True)
        scaled = embedded[:, :depth] * lax.rsqrt(mean + EPS) * gain_ref[...]
        act_ref[low + start : low + start + ROW_STEP] = gelu(scaled).astype(jnp.bfloat16)


def convolve(blocks, w_ref):
    second = lax.axis_index("strand")
    total = None
    for tap, block in enumerate(blocks):
        weight = w_ref[tap + second * (2 - 2 * tap)]
        part = jnp.dot(block, weight, preferred_element_type=jnp.float32)
        total = part if total is None else total + part
    return total


def first_kernel(row_count, length, tok_ref, table_ref, gain_ref, w_any, out_ref, kept_ref, w_ref, act_ref, sem):
    copy = pltpu.make_async_copy(w_any, w_ref, sem)
    copy.start()
    taps = base_taps(tok_ref, row_count, length, 0, 3 * DILATION)
    hot = one_hot(taps, lax.axis_index("strand"), table_ref.shape[0]).astype(jnp.bfloat16)
    activate(hot, table_ref, gain_ref, act_ref, 0)
    kept_ref[...] = act_ref[DILATION:]
    copy.wait()
    blocks = [act_ref[t * DILATION : (t + 1) * DILATION] for t in range(3)]
    out_ref[...] = convolve(blocks, w_ref).astype(jnp.bfloat16)


def next_kernel(row_count, length, low, tok_ref, table_ref, gain_ref, kept_ref, w_ref, out_ref, now_ref, act_ref):
    taps = base_taps(tok_ref, row_count, length, low + 2 * DILATION, DILATION)
    hot = one_hot(taps, lax.axis_index("strand"), table_ref.shape[0]).astype(jnp.bfloat16)
    activate(hot, table_ref, gain_ref, act_ref, 0)
    blocks = [kept_ref[:DILATION], kept_ref[DILATION:], act_ref[...]]
    now_ref[:DILATION] = kept_ref[DILATION:]
    now_ref[DILATION:] = act_ref[...]
    out_ref[...] = convolve(blocks, w_ref).astype(jnp.bfloat16)


def own_kernel(length, places, piece_rows, *refs):
    tok_ref, table_ref, plain_ref, gain_ref, w_ref = refs[:5]
    pieces = refs[5 : 5 + len(places)]
    out_ref, res_ref, point_ref, act_ref, sems = refs[5 + len(places) :]
    row_count = out_ref.shape[0]
    count, groups = lax.axis_size("dp"), lax.axis_size("groups")
    me, group = lax.axis_index("dp"), lax.axis_index("groups")
    copies = []
    for index, (step, turn, all_groups) in enumerate(places):
        place = lax.rem(me + step, count) * (piece_rows * groups)
        if not all_groups:
            place = place + lax.rem(group + turn, groups) * piece_rows
        target = pl.ds(pl.multiple_of(place, 16), pieces[index].shape[0])
        copies.append(pltpu.make_async_copy(pieces[index], point_ref.at[target], sems.at[index]))
        copies[-1].start()
    second = lax.axis_index("strand")
    taps = base_taps(tok_ref, row_count, length, 0, row_count + 2 * DILATION)
    hot = one_hot(taps, second, table_ref.shape[0])
    here = slice(DILATION, DILATION + row_count)
    both = hot[here] + one_hot(taps[:, here], 1 - second, table_ref.shape[0])
    res_ref[...] = jnp.dot(
        both.astype(jnp.bfloat16), plain_ref[...], preferred_element_type=jnp.float32
    )
    activate(hot.astype(jnp.bfloat16), table_ref, gain_ref, act_ref, 0)
    for low in range(0, row_count, DILATION):
        blocks = [act_ref[low + t * DILATION : low + (t + 1) * DILATION] for t in range(3)]
        out_ref[low : low + DILATION] = convolve(blocks, w_ref)
    for copy in copies:
        copy.wait()


def middle_kernel(low, own_ref, gain_ref, *refs):
    out_ref = refs[-1]
    for start in range(0, out_ref.shape[0], ROW_STEP):
        total = own_ref[low + start : low + start + ROW_STEP]
        for ref in refs[:-1]:
            total = total + ref[start : start + ROW_STEP].astype(jnp.float32)
        mean = jnp.mean(total * total, axis=-1, keepdims=True)
        value = gelu(total * lax.rsqrt(mean + EPS) * gain_ref[...])
        out_ref[start : start + ROW_STEP] = value.astype(jnp.bfloat16)


def final_kernel(low, mine_ref, other_ref, res_ref, point_ref, *refs):
    out_ref = refs[-1]
    total = mine_ref[...].astype(jnp.float32) + other_ref[...].astype(jnp.float32)
    branch = jnp.dot(
        total.astype(jnp.bfloat16), point_ref[...], preferred_element_type=jnp.float32
    )
    rows = slice(low, low + DILATION)
    out_ref[...] = (0.5 * (branch + res_ref[rows])).astype(jnp.bfloat16)


def cost(micros):
    return pl.CostEstimate(flops=0, bytes_accessed=int(3.6e6 * micros), transcendentals=0)


def per_device(tokens, stem_table, conv_weight, gain_in, gain_mid, point_weight):
    row_count = tokens.shape[1]
    tap_total, kinds, width = stem_table.shape
    depth, inner = conv_weight.shape[1:]
    count, groups = lax.axis_size("dp"), lax.axis_size("groups")
    length = row_count * lax.axis_size("seq")
    me, group, strand = (lax.axis_index(axis) for axis in ("dp", "groups", "strand"))
    half = width // 2
    vmem = pl.BlockSpec(memory_space=pltpu.VMEM)
    anywhere = pl.BlockSpec(memory_space=pl.ANY)
    bf16, f32 = jnp.bfloat16, jnp.float32
    params = pltpu.CompilerParams(vmem_limit_bytes=24 * MIB)

    base_ids = tokens[0]
    low = lax.ppermute(base_ids[row_count - REACH :], "seq", shifted_pairs("seq", 1))
    high = lax.ppermute(base_ids[:REACH], "seq", shifted_pairs("seq", -1))
    near = jnp.concatenate([low, base_ids, high])[None]
    sequences = [near] + [
        lax.ppermute(near, "dp", ring_pairs("dp", -step)) for step in range(1, count)
    ]

    table_rows = 16 * kinds
    flat = jnp.pad(
        stem_table.reshape(tap_total * kinds, width), ((0, table_rows - tap_total * kinds), (0, 0))
    )
    table = lax.dynamic_slice_in_dim(
        jnp.concatenate([flat, flat], axis=1), me * depth, width, axis=1
    )
    plain = lax.dynamic_slice_in_dim(flat, strand * half, half, axis=1)
    gain_here = lax.dynamic_slice_in_dim(gain_in, me * depth, depth)[None]

    columns = lax.dynamic_slice_in_dim(point_weight, strand * half, half, axis=1)
    piece_rows = point_weight.shape[0] // groups
    piece = lax.dynamic_slice_in_dim(columns, group * piece_rows, piece_rows, axis=0)
    places, pieces = [(0, 0, True)], [columns]
    for step in range(1, count):
        crossed = lax.ppermute(piece, "dp", ring_pairs("dp", -step))
        for turn in range(groups):
            places.append((step, turn, False))
            pieces.append(
                lax.ppermute(crossed, "groups", ring_pairs("groups", -turn)) if turn else crossed
            )

    w_here = conv_weight
    received = []
    for step in range(1, count):
        tok = sequences[step]
        kept_shape = jax.ShapeDtypeStruct((2 * DILATION, depth), bf16)
        part_shape = jax.ShapeDtypeStruct((DILATION, inner), bf16)
        part, kept, w_here = pl.pallas_call(
            functools.partial(first_kernel, row_count, length),
            out_shape=[part_shape, kept_shape, jax.ShapeDtypeStruct(conv_weight.shape, bf16)],
            in_specs=[vmem] * 3 + [pl.BlockSpec(memory_space=pltpu.HBM)],
            out_specs=[vmem] * 3,
            scratch_shapes=[
                pltpu.VMEM((3 * DILATION, depth), bf16),
                pltpu.SemaphoreType.DMA,
            ],
            compiler_params=params,
            cost_estimate=cost(3),
            name="conv_first",
        )(tok, table, gain_here, pltpu.with_memory_space_constraint(conv_weight, pltpu.HBM))
        parts = [lax.ppermute(part, "dp", ring_pairs("dp", step))]
        for start in range(DILATION, row_count, DILATION):
            part, kept = pl.pallas_call(
                functools.partial(next_kernel, row_count, length, start),
                out_shape=[part_shape, kept_shape],
                in_specs=[vmem] * 5,
                out_specs=[vmem] * 2,
                scratch_shapes=[pltpu.VMEM((DILATION, depth), bf16)],
                compiler_params=params,
                cost_estimate=cost(2),
                name="conv_next",
            )(tok, table, gain_here, kept, w_here)
            parts.append(lax.ppermute(part, "dp", ring_pairs("dp", step)))
        received.append(parts)

    own, res, point = pl.pallas_call(
        functools.partial(own_kernel, length, places, piece_rows),
        out_shape=[
            jax.ShapeDtypeStruct((row_count, inner), f32),
            jax.ShapeDtypeStruct((row_count, half), f32),
            jax.ShapeDtypeStruct((inner, half), bf16),
        ],
        in_specs=[vmem] * 5 + [anywhere] * len(pieces),
        out_specs=[vmem] * 3,
        scratch_shapes=[
            pltpu.VMEM((row_count + 2 * DILATION, depth), bf16),
            pltpu.SemaphoreType.DMA((len(pieces),)),
        ],
        compiler_params=params,
        cost_estimate=cost(5),
        name="conv_own",
    )(near, table, plain, gain_here, w_here, *pieces)

    out = None
    for index, start in enumerate(range(0, row_count, DILATION)):
        middle = pl.pallas_call(
            functools.partial(middle_kernel, start),
            out_shape=jax.ShapeDtypeStruct((DILATION, inner), bf16),
            in_specs=[vmem] * (count + 1),
            out_specs=vmem,
            compiler_params=params,
            cost_estimate=cost(0.5),
            name="middle",
        )(own, gain_mid[None], *[parts[index] for parts in received])
        other = lax.ppermute(middle, "strand", ring_pairs("strand", 1))
        operands = [middle, other, res, point] + ([] if out is None else [out])
        out = pl.pallas_call(
            functools.partial(final_kernel, start),
            grid=(1,),
            out_shape=jax.ShapeDtypeStruct((row_count, half), bf16),
            in_specs=[vmem] * 4 + [anywhere] * (len(operands) - 4),
            out_specs=pl.BlockSpec((DILATION, half), lambda i, index=index: (index, 0)),
            input_output_aliases={} if out is None else {4: 0},
            compiler_params=params,
            cost_estimate=cost(0.7),
            name="final",
        )(*operands)
    return out[None]


def solution(mesh):
    return jax.shard_map(
        per_device,
        mesh=mesh,
        in_specs=(P(("groups", "dp"), "seq"), P(), P(None, "dp", None), P(), P(), P("dp", None)),
        out_specs=P(("groups", "dp"), "seq", "strand"),
        check_vma=False,
    )
```

time: 264 us -> 41.9 us (0.16)
  waiting for transfers between devices: 206 us -> 11.9 us
  between operations: 13.6 us -> 0.16 us
  matrix products: 13 us -> 0 us
  Pallas kernels: 0 us -> 12.5 us
  starting transfers between devices: 20.9 us -> 13.1 us
  other arithmetic: 4.3 us -> 0.78 us
  local copies, waits for them, and re-layouts: 5.97 us -> 3.09 us
    ppermute x9, waiting for transfers between devices: 122 us -> 11.9 us  [the longest x1 5.38 us: per_device(): lax.ppermute(crossed, 'groups', ring_pairs('groups', -turn))]
    all_gather x2 -> x0, waiting for transfers between devices: 82.4 us -> none  [the longest x1 53.9 us: per_device(): weight_block = lax.all_gather(conv_weight, 'dp', axis=1, tiled=True)]
    dot_general x5 -> x0, matrix products: 13 us -> none  [the longest x3 8.55 us: per_device(): jnp.dot(tap_slices, weight_block[tap_position], preferred_element_type=jn...]
    pallas_call x0 -> x7, Pallas kernels: none -> 12.5 us  [the longest x1 4.24 us: per_device(): pl.pallas_call(functools.partial(own_kernel, length, places, piece_rows),...]
    ppermute x9, starting transfers between devices: 20.8 us -> 13.1 us  [the longest x1 4.93 us: per_device(): lax.ppermute(base_ids[row_count - REACH:], 'seq', shifted_pairs('seq', 1))]
  transfers between devices with their start and end apart: 11 -> 9, of which waited for: 9 -> 5; matrix products, arithmetic and copies ran while one was open for 5% -> 7% of each run, Pallas kernels for 0% -> 27%
where the time goes in v2:
time: 41.9 us; the launch traced here: 41.6 us
  starting transfers between devices  13.1 us (31%)
  Pallas kernels  12.5 us (30%)
  waiting for transfers between devices  11.9 us (28%)
  local copies, waits for them, and re-layouts  3.09 us (7%)
  other arithmetic  0.78 us (2%)
    ppermute x1, waiting for transfers between devices, per_device(): lax.ppermute(crossed, 'groups', ring_pairs('groups', -turn))  5.38 us
    ppermute x1, starting transfers between devices, per_device(): lax.ppermute(base_ids[row_count - REACH:], 'seq', shifted_pairs('seq', 1))  4.93 us
    pallas_call x1, Pallas kernels, per_device(): pl.pallas_call(functools.partial(own_kernel, length, places, piece_rows),...  4.24 us
    ppermute x1, waiting for transfers between devices, per_device(): lax.ppermute(near, 'dp', ring_pairs('dp', -step))  3.18 us
    pallas_call x1, Pallas kernels, per_device(): pl.pallas_call(functools.partial(first_kernel, row_count, length), out_sh...  3.17 us
    pallas_call x2, Pallas kernels, per_device(): pl.pallas_call(functools.partial(final_kernel, start), grid=(1,), out_sha...  2.5 us
    ppermute x1, waiting for transfers between devices, per_device(): parts.append(lax.ppermute(part, 'dp', ring_pairs('dp', step)))  2.48 us
    pallas_call x1, Pallas kernels, per_device(): pl.pallas_call(functools.partial(next_kernel, row_count, length, start),...  1.83 us
  transfers between devices with their start and end apart: 9, of which 5 were waited for; matrix products, arithmetic and copies ran while one was open for 7% of the time, Pallas kernels for 27%

profile of v2, /device:TPU:0, one launch (start us, length us, event | category | flops | bytes accessed | tf_op | source)
XLA Modules:
  0.0 41.6 jit_solution(1624086302629303683)
XLA Ops:
  0.0 0.8 %slice_reduce_fusion.1 = (s32[384]{0:T(512)S(1)}, s32[384]{0:T(512)S(1)}) fusion(s32[1,512]{1,0:T(1,128)} %param.6), kind=kLoop, calls=%fused_computation.5 | loop fusion | bytes 6144 | tf_op jit(solution)/shard_map/slice | solution.py:169
  0.8 4.9 %collective-permute-start = (s32[384]{0:T(512)S(1)}, s32[384]{0:T(512)S(1)}, u32[]{:S(2)}, u32[]{:S(2)}) collective-permute-start(s32[384]{0:T(512)S(1)} %get-tuple-element.19), channel_id=1, source_target_pairs={{0,4},{4,8},{8,12},{1,5},{5,9},{9,13},{2,6},{6,10},{10,14},{3,7},{... | collective-permute-start | bytes 4616 | tf_op jit(solution)/shard_map/ppermute | solution.py:169
  5.7 1.3 %collective-permute-start.1 = (s32[384]{0:T(512)S(1)}, s32[384]{0:T(512)S(1)}, u32[]{:S(2)}, u32[]{:S(2)}) collective-permute-start(s32[384]{0:T(512)S(1)} %get-tuple-element.20), channel_id=1, source_target_pairs={{4,0},{8,4},{12,8},{5,1},{9,5},{13,9},{6,2},{10,6},{14,10},{7,3},{... | collective-permute-start | bytes 4616 | tf_op jit(solution)/shard_map/ppermute | solution.py:170
  7.0 1.2 %dynamic_slice.19 = bf16[192,768]{1,0:T(8,128)(2,1)S(1)} dynamic-slice(bf16[384,1536]{1,0:T(8,128)(2,1)} %param.11, s32[]{:T(128)S(6)} %select_n.21, s32[]{:T(128)S(6)} %select_n.22), dynamic_slice_sizes={192,768} | dynamic-slice | bytes 589828 | tf_op jit(solution)/shard_map/dynamic_slice | solution.py:188
  8.2 1.6 %collective-permute-start.3 = (bf16[192,768]{1,0:T(8,128)(2,1)S(1)}, bf16[192,768]{1,0:T(8,128)(2,1)S(1)}, u32[]{:S(2)}, u32[]{:S(2)}) collective-permute-start(bf16[192,768]{1,0:T(8,128)(2,1)S(1)} %dynamic_slice.19), channel_id=1, source_target_pairs={{0,2},{2,0},{1,3},{3,1},{4,6},{6,4},{5,7},{7,5},{8,10},{10,8},{9,1... | collective-permute-start | bytes 884744 | tf_op jit(solution)/shard_map/ppermute | solution.py:191
  9.7 1.0 %reshape.5 = bf16[60,1536]{1,0:T(8,128)(2,1)S(1)} reshape(bf16[15,4,1536]{2,1,0:T(4,128)(2,1)} %param.7) | data formatting | bytes 368640 | tf_op jit(solution)/shard_map/reshape | solution.py:178
  10.8 0.4 %collective-permute-done.1 = s32[384]{0:T(512)S(1)} collective-permute-done((s32[384]{0:T(512)S(1)}, s32[384]{0:T(512)S(1)}, u32[]{:S(2)}, u32[]{:S(2)}) %collective-permute-start.1) | collective-permute-done | bytes 1568 | tf_op jit(solution)/shard_map/ppermute | solution.py:170
  11.2 0.7 %pad_add_fusion = s32[1280]{0:T(1024)S(1)} fusion(s32[384]{0:T(512)S(1)} %collective-permute-done.1, s32[512]{0:T(512)} %bitcast.2, s32[384]{0:T(512)S(1)} %collective-permute-done), kind=kLoop, calls=%fused_computation.3 | loop fusion | flops 2560 | bytes 10240 | tf_op jit(solution)/shard_map/concatenate | solution.py:171
  11.9 1.6 %collective-permute-start.2 = (s32[1,1280]{1,0:T(1,128)S(1)}, s32[1,1280]{1,0:T(1,128)S(1)}, u32[]{:S(2)}, u32[]{:S(2)}) collective-permute-start(s32[1,1280]{1,0:T(1,128)S(1)} %broadcast_in_dim.13.refs_0_), channel_id=1, source_target_pairs={{0,2},{2,0},{1,3},{3,1},{4,6},{6,4},{5,7},{7,5},{8,10},{10,8},{9,1... | collective-permute-start | bytes 15368 | tf_op jit(solution)/shard_map/ppermute | solution.py:173
  13.4 0.1 fusion.table_ref.refs_1_
  13.6 3.2 %collective-permute-done.2.tok_ref = s32[1,1280]{1,0:T(1,128)S(1)} collective-permute-done((s32[1,1280]{1,0:T(1,128)S(1)}, s32[1,1280]{1,0:T(1,128)S(1)}, u32[]{:S(2)}, u32[]{:S(2)}) %collective-permute-start.2) | collective-permute-done | bytes 5152 | tf_op jit(solution)/shard_map/ppermute | solution.py:173
  16.8 3.2 %conv_first.1 = (bf16[256,768]{1,0:T(8,128)(2,1)S(1)}, bf16[512,768]{1,0:T(8,128)(2,1)S(1)}, bf16[3,768,768]{2,1,0:T(8,128)(2,1)S(1)}) custom-call(s32[1,1280]{1,0:T(1,128)S(1)} %collective-permute-done.2.tok_ref, bf16[64,1536]{1,0:T(8,128)(2,1)S(1)} %fusion.table_ref.refs_1_, f32[1,768]{1,0:T(1,128)S(1)} %broadcast_in_dim.14.gain_ref.refs_3_, ...), custom_call_target="tpu_custom_call" | custom-call | bytes 10800000 | tf_op jit(solution)/shard_map/conv_first/pallas_call | solution.py:204
  20.0 1.6 %collective-permute-start.7 = (bf16[256,768]{1,0:T(8,128)(2,1)S(1)}, bf16[256,768]{1,0:T(8,128)(2,1)S(1)}, u32[]{:S(2)}, u32[]{:S(2)}) collective-permute-start(bf16[256,768]{1,0:T(8,128)(2,1)S(1)} %get-tuple-element.18), channel_id=1, source_target_pairs={{0,2},{2,0},{1,3},{3,1},{4,6},{6,4},{5,7},{7,5},{8,10},{10,8},{9,1... | collective-permute-start | bytes 1179656 | tf_op jit(solution)/shard_map/ppermute | solution.py:217
  21.6 1.8 %conv_next.1 = (bf16[256,768]{1,0:T(8,128)(2,1)S(1)}, bf16[512,768]{1,0:T(8,128)(2,1)}) custom-call(s32[1,1280]{1,0:T(1,128)S(1)} %collective-permute-done.2.tok_ref, bf16[64,1536]{1,0:T(8,128)(2,1)S(1)} %fusion.table_ref.refs_1_, f32[1,768]{1,0:T(1,128)S(1)} %broadcast_in_dim.14.gain_ref.refs_3_, bf16[512,768]{1,0:T(8,128)(2,1)S(1)} %get-tuple-element.14.kept_ref, ...), custom_call_target="tpu_custom_call" | custom-call | bytes 7200000 | tf_op jit(solution)/shard_map/conv_next/pallas_call | solution.py:219
  23.4 0.5 %collective-permute-start.5 = (bf16[256,768]{1,0:T(8,128)(2,1)S(1)}, bf16[256,768]{1,0:T(8,128)(2,1)S(1)}, u32[]{:S(2)}, u32[]{:S(2)}) collective-permute-start(bf16[256,768]{1,0:T(8,128)(2,1)S(1)} %get-tuple-element.15), channel_id=1, source_target_pairs={{0,2},{2,0},{1,3},{3,1},{4,6},{6,4},{5,7},{7,5},{8,10},{10,8},{9,1... | collective-permute-start | bytes 1179656 | tf_op jit(solution)/shard_map/ppermute | solution.py:229
  23.9 1.5 %collective-permute-start.4 = (bf16[192,768]{1,0:T(8,128)(2,1)S(1)}, bf16[192,768]{1,0:T(8,128)(2,1)S(1)}, u32[]{:S(2)}, u32[]{:S(2)}) collective-permute-start(bf16[192,768]{1,0:T(8,128)(2,1)S(1)} %collective-permute-done.3.refs_6_), channel_id=1, source_target_pairs={{0,16},{16,0},{1,17},{17,1},{2,18},{18,2},{3,19},{19,3},{4,20},{20... | collective-permute-start | bytes 884744 | tf_op jit(solution)/shard_map/ppermute | solution.py:195
  25.5 5.4 %collective-permute-done.4.refs_7_ = bf16[192,768]{1,0:T(8,128)(2,1)S(1)} collective-permute-done((bf16[192,768]{1,0:T(8,128)(2,1)S(1)}, bf16[192,768]{1,0:T(8,128)(2,1)S(1)}, u32[]{:S(2)}, u32[]{:S(2)}) %collective-permute-start.4) | collective-permute-done | bytes 294944 | tf_op jit(solution)/shard_map/ppermute | solution.py:195
  30.9 4.2 %conv_own.1 = (f32[512,768]{1,0:T(8,128)S(1)}, f32[512,768]{1,0:T(8,128)S(1)}, bf16[768,768]{1,0:T(8,128)(2,1)S(1)}) custom-call(s32[1,1280]{1,0:T(1,128)S(1)} %broadcast_in_dim.13.refs_0_, bf16[64,1536]{1,0:T(8,128)(2,1)S(1)} %fusion.table_ref.refs_1_, bf16[64,768]{1,0:T(8,128)(2,1)S(1)} %constant_dynamic-slice_fusion.1.refs_2_, ...), custom_call_target="tpu_custom_call" | custom-call | bytes 18000000 | tf_op jit(solution)/shard_map/conv_own/pallas_call | solution.py:232
  35.2 0.4 middle.3.mine_ref
  35.6 2.5 %collective-permute-done.5.refs_0_ = bf16[256,768]{1,0:T(8,128)(2,1)S(1)} collective-permute-done((bf16[256,768]{1,0:T(8,128)(2,1)S(1)}, bf16[256,768]{1,0:T(8,128)(2,1)S(1)}, u32[]{:S(2)}, u32[]{:S(2)}) %collective-permute-start.5) | collective-permute-done | bytes 393248 | tf_op jit(solution)/shard_map/ppermute | solution.py:229
  38.1 0.4 middle.2.mine_ref
  38.6 1.3 %final.2.refs_0_ = bf16[512,768]{1,0:T(8,128)(2,1)} custom-call(bf16[256,768]{1,0:T(8,128)(2,1)S(1)} %middle.3.mine_ref, bf16[256,768]{1,0:T(8,128)(2,1)S(1)} %collective-permute-done.8.other_ref, f32[512,768]{1,0:T(8,128)S(1)} %get-tuple-element.16.res_ref, bf16[768,768]{1,0:T(8,128)(2,1)S(1)} %get-tuple-element.17.point_ref), custom_call_target="tpu_custom_call" | custom-call | bytes 2520000 | tf_op jit(solution)/shard_map/final/pallas_call | solution.py:263
  39.9 0.4 %collective-permute-done.6.other_ref = bf16[256,768]{1,0:T(8,128)(2,1)S(1)} collective-permute-done((bf16[256,768]{1,0:T(8,128)(2,1)S(1)}, bf16[256,768]{1,0:T(8,128)(2,1)S(1)}, u32[]{:S(2)}, u32[]{:S(2)}) %collective-permute-start.6) | collective-permute-done | bytes 393248 | tf_op jit(solution)/shard_map/ppermute | solution.py:261
  40.3 1.3 %final.3 = bf16[512,768]{1,0:T(8,128)(2,1)} custom-call(bf16[256,768]{1,0:T(8,128)(2,1)S(1)} %middle.2.mine_ref, bf16[256,768]{1,0:T(8,128)(2,1)S(1)} %collective-permute-done.6.other_ref, f32[512,768]{1,0:T(8,128)S(1)} %get-tuple-element.16.res_ref, bf16[768,768]{1,0:T(8,128)(2,1)S(1)} %get-tuple-element.17.point_ref, ...), custom_call_target="tpu_custom_call", output_to_operand_aliasing={{}: (4, {})} | custom-call | bytes 2520000 | tf_op jit(solution)/shard_map/final/pallas_call | solution.py:263
  (19 shorter events, 0.3 us)
Async XLA Ops:
  0.0 13.5 %copy-start.2 = (f32[1536]{0:T(1024)S(1)}, f32[1536]{0:T(1024)}, u32[]{:S(2)}) copy-start(f32[1536]{0:T(1024)} %param.9) | copy-start | bytes 18436
  0.8 10.0 %collective-permute-start = (s32[384]{0:T(512)S(1)}, s32[384]{0:T(512)S(1)}, u32[]{:S(2)}, u32[]{:S(2)}) collective-permute-start(s32[384]{0:T(512)S(1)} %get-tuple-element.19), channel_id=1, source_target_pairs={{0,4},{4,8},{8,12},{1,5},{5,9},{9,13},{2,6},{6,10},{10,14},{3,7},{... | collective-permute-start | bytes 4616 | tf_op jit(solution)/shard_map/ppermute | solution.py:169
  5.7 5.5 %collective-permute-start.1 = (s32[384]{0:T(512)S(1)}, s32[384]{0:T(512)S(1)}, u32[]{:S(2)}, u32[]{:S(2)}) collective-permute-start(s32[384]{0:T(512)S(1)} %get-tuple-element.20), channel_id=1, source_target_pairs={{4,0},{8,4},{12,8},{5,1},{9,5},{13,9},{6,2},{10,6},{14,10},{7,3},{... | collective-permute-start | bytes 4616 | tf_op jit(solution)/shard_map/ppermute | solution.py:170
  8.2 15.7 %collective-permute-start.3 = (bf16[192,768]{1,0:T(8,128)(2,1)S(1)}, bf16[192,768]{1,0:T(8,128)(2,1)S(1)}, u32[]{:S(2)}, u32[]{:S(2)}) collective-permute-start(bf16[192,768]{1,0:T(8,128)(2,1)S(1)} %dynamic_slice.19), channel_id=1, source_target_pairs={{0,2},{2,0},{1,3},{3,1},{4,6},{6,4},{5,7},{7,5},{8,10},{10,8},{9,1... | collective-permute-start | bytes 884744 | tf_op jit(solution)/shard_map/ppermute | solution.py:191
  11.9 4.9 %collective-permute-start.2 = (s32[1,1280]{1,0:T(1,128)S(1)}, s32[1,1280]{1,0:T(1,128)S(1)}, u32[]{:S(2)}, u32[]{:S(2)}) collective-permute-start(s32[1,1280]{1,0:T(1,128)S(1)} %broadcast_in_dim.13.refs_0_), channel_id=1, source_target_pairs={{0,2},{2,0},{1,3},{3,1},{4,6},{6,4},{5,7},{7,5},{8,10},{10,8},{9,1... | collective-permute-start | bytes 15368 | tf_op jit(solution)/shard_map/ppermute | solution.py:173
  20.0 15.2 %collective-permute-start.7 = (bf16[256,768]{1,0:T(8,128)(2,1)S(1)}, bf16[256,768]{1,0:T(8,128)(2,1)S(1)}, u32[]{:S(2)}, u32[]{:S(2)}) collective-permute-start(bf16[256,768]{1,0:T(8,128)(2,1)S(1)} %get-tuple-element.18), channel_id=1, source_target_pairs={{0,2},{2,0},{1,3},{3,1},{4,6},{6,4},{5,7},{7,5},{8,10},{10,8},{9,1... | collective-permute-start | bytes 1179656 | tf_op jit(solution)/shard_map/ppermute | solution.py:217
  21.6 3.9 %copy-start.1 = (f32[768]{0:T(1024)S(1)}, f32[768]{0:T(1024)}, u32[]{:S(2)}) copy-start(f32[768]{0:T(1024)} %param.10) | copy-start | bytes 9220
  21.6 3.9 %copy-start = (bf16[384,1536]{1,0:T(8,128)(2,1)S(1)}, bf16[384,1536]{1,0:T(8,128)(2,1)}, u32[]{:S(2)}) copy-start(bf16[384,1536]{1,0:T(8,128)(2,1)} %param.11) | copy-start | bytes 3538948
  23.4 14.7 %collective-permute-start.5 = (bf16[256,768]{1,0:T(8,128)(2,1)S(1)}, bf16[256,768]{1,0:T(8,128)(2,1)S(1)}, u32[]{:S(2)}, u32[]{:S(2)}) collective-permute-start(bf16[256,768]{1,0:T(8,128)(2,1)S(1)} %get-tuple-element.15), channel_id=1, source_target_pairs={{0,2},{2,0},{1,3},{3,1},{4,6},{6,4},{5,7},{7,5},{8,10},{10,8},{9,1... | collective-permute-start | bytes 1179656 | tf_op jit(solution)/shard_map/ppermute | solution.py:229
  23.9 7.0 %collective-permute-start.4 = (bf16[192,768]{1,0:T(8,128)(2,1)S(1)}, bf16[192,768]{1,0:T(8,128)(2,1)S(1)}, u32[]{:S(2)}, u32[]{:S(2)}) collective-permute-start(bf16[192,768]{1,0:T(8,128)(2,1)S(1)} %collective-permute-done.3.refs_6_), channel_id=1, source_target_pairs={{0,16},{16,0},{1,17},{17,1},{2,18},{18,2},{3,19},{19,3},{4,20},{20... | collective-permute-start | bytes 884744 | tf_op jit(solution)/shard_map/ppermute | solution.py:195
  35.6 3.0 %collective-permute-start.8 = (bf16[256,768]{1,0:T(8,128)(2,1)S(1)}, bf16[256,768]{1,0:T(8,128)(2,1)S(1)}, u32[]{:S(2)}, u32[]{:S(2)}) collective-permute-start(bf16[256,768]{1,0:T(8,128)(2,1)S(1)} %middle.3.mine_ref), channel_id=1, source_target_pairs={{0,1},{1,0},{2,3},{3,2},{4,5},{5,4},{6,7},{7,6},{8,9},{9,8},{10,11... | collective-permute-start | bytes 1179656 | tf_op jit(solution)/shard_map/ppermute | solution.py:261
  38.5 1.8 %collective-permute-start.6 = (bf16[256,768]{1,0:T(8,128)(2,1)S(1)}, bf16[256,768]{1,0:T(8,128)(2,1)S(1)}, u32[]{:S(2)}, u32[]{:S(2)}) collective-permute-start(bf16[256,768]{1,0:T(8,128)(2,1)S(1)} %middle.2.mine_ref), channel_id=1, source_target_pairs={{0,1},{1,0},{2,3},{3,2},{4,5},{5,4},{6,7},{7,6},{8,9},{9,8},{10,11... | collective-permute-start | bytes 1179656 | tf_op jit(solution)/shard_map/ppermute | solution.py:261

commit v3 on v2

v3 whole, which is shorter than its diff:
```python
import functools

import jax
import jax.numpy as jnp
from jax import lax
from jax.experimental import pallas as pl
from jax.experimental.pallas import tpu as pltpu
from jax.sharding import PartitionSpec as P

DILATION = 256
EPS = 1e-06
ROW_STEP = 128
CHUNKS = ((0, 64), (128, 128), (64, 64))
KINDS = 4
FLOPS = {"early": 0.1, "sent": 1.0, "own": 10.0, "middle": 0.3, "final": 10.0}
MIB = 2**20


def ring_pairs(axis, distance):
    count = lax.axis_size(axis)
    return [(i, (i + distance) % count) for i in range(count)]


def base_taps(tok_ref, step, row_count):
    count, blocks = lax.axis_size("dp"), lax.axis_size("seq")
    here = lax.axis_index("seq")
    first = lax.rem(lax.axis_index("dp") + step, count) * blocks
    sides = [jnp.maximum(here - 1, 0), here, jnp.minimum(here + 1, blocks - 1)]
    bases = jnp.concatenate([tok_ref[pl.ds(first + side, 1), :] for side in sides], axis=1)
    width, span = 3 * row_count, row_count + 2 * DILATION
    spread = jnp.broadcast_to(bases, (16, width))
    start = width - (row_count - DILATION + 8)
    taps = pltpu.roll(spread, start, 1, stride=1, stride_axis=0)[:, :span]
    place = lax.broadcasted_iota(jnp.int32, (16, span), 1) + (here * row_count - DILATION)
    source = place + 8 - lax.broadcasted_iota(jnp.int32, (16, span), 0)
    length = blocks * row_count
    inside = (place >= 0) & (place < length) & (source >= 0) & (source < length)
    return jnp.where(inside, taps, -1).astype(jnp.float32).astype(jnp.bfloat16)


def one_hot(taps, second, table_rows):
    row = lax.broadcasted_iota(jnp.int32, (table_rows, 16), 0) // KINDS
    column = lax.broadcasted_iota(jnp.int32, (table_rows, 16), 1)
    chosen = (column == 15 - row + second * (2 * row - 14)).astype(jnp.float32)
    values = jnp.dot(chosen.astype(jnp.bfloat16), taps, preferred_element_type=jnp.float32)
    base = lax.broadcasted_iota(jnp.int32, values.shape, 0) % KINDS
    base = base + second * (KINDS - 1 - 2 * base)
    return (values == base.astype(jnp.float32)).astype(jnp.float32).T


def gelu(x):
    inner = x * (0.7978845608028654 + 0.035677408136300125 * (x * x))
    half = 0.5 * x
    return half + half * jnp.tanh(inner)


def activate(hot, table_ref, gain_ref, act_ref):
    depth = gain_ref.shape[1]
    for start in range(0, hot.shape[0], ROW_STEP):
        embedded = jnp.dot(
            hot[start : start + ROW_STEP], table_ref[...], preferred_element_type=jnp.float32
        )
        mean = jnp.mean(embedded * embedded, axis=-1, keepdims=True)
        scaled = embedded[:, :depth] * lax.rsqrt(mean + EPS) * gain_ref[...]
        act_ref[start : start + ROW_STEP] = gelu(scaled).astype(jnp.bfloat16)


def convolve(blocks, w_ref):
    second = lax.axis_index("strand")
    total = None
    for tap, block in enumerate(blocks):
        weight = w_ref[tap + second * (2 - 2 * tap)]
        part = jnp.dot(block, weight, preferred_element_type=jnp.float32)
        total = part if total is None else total + part
    return total


def chunk_kernel(step, low, size, row_count, first, operand_count, *refs):
    tok_ref, table_ref, gain_ref, w_ref = refs[:4]
    out_ref = refs[operand_count]
    if first:
        kept_ref, act_ref, sem = refs[-3:]
        copy = pltpu.make_async_copy(w_ref, kept_ref, sem)
        copy.start()
        w_ref = kept_ref
    else:
        act_ref = refs[-1]
    taps = base_taps(tok_ref, step, row_count)
    hot = one_hot(taps, lax.axis_index("strand"), table_ref.shape[0])
    blocks = row_count // DILATION
    pieces = [hot[b * DILATION + low :][:size] for b in range(blocks + 2)]
    activate(jnp.concatenate(pieces).astype(jnp.bfloat16), table_ref, gain_ref, act_ref)
    if first:
        copy.wait()
    parts = [act_ref[t * size : (t + blocks) * size] for t in range(3)]
    out_ref[...] = convolve(parts, w_ref).astype(jnp.bfloat16)


def rows_of(ref, low, size):
    starts = range(low, ref.shape[0], DILATION)
    return jnp.concatenate([ref[start : start + size] for start in starts])


def middle_of(own_ref, gain_ref, parts, low, size):
    total = rows_of(own_ref, low, size)
    for ref in parts:
        total = total + ref[...].astype(jnp.float32)
    mean = jnp.mean(total * total, axis=-1, keepdims=True)
    return gelu(total * lax.rsqrt(mean + EPS) * gain_ref[...]).astype(jnp.bfloat16)


def own_kernel(chunk, *refs):
    tok_ref, table_ref, plain_ref, gain_ref, w_ref, gain_mid_ref = refs[:6]
    parts, (out_ref, res_ref, middle_ref, act_ref) = refs[6:-4], refs[-4:]
    row_count = out_ref.shape[0]
    second = lax.axis_index("strand")
    taps = base_taps(tok_ref, 0, row_count)
    hot = one_hot(taps, second, table_ref.shape[0])
    here = slice(DILATION, DILATION + row_count)
    both = hot[here] + one_hot(taps[:, here], 1 - second, table_ref.shape[0])
    res_ref[...] = jnp.dot(
        both.astype(jnp.bfloat16), plain_ref[...], preferred_element_type=jnp.float32
    )
    activate(hot.astype(jnp.bfloat16), table_ref, gain_ref, act_ref)
    blocks = [act_ref[t * DILATION : t * DILATION + row_count] for t in range(3)]
    out_ref[...] = convolve(blocks, w_ref)
    middle_ref[...] = middle_of(out_ref, gain_mid_ref, parts, *chunk)


def middle_kernel(low, size, count, places, piece_rows, own_ref, gain_ref, *refs):
    parts, pieces = refs[:count], refs[count : count + len(places)]
    out_ref = refs[-3] if places else refs[-1]
    copies = []
    if places:
        point_ref, sems = refs[-2:]
        ranks, groups = lax.axis_size("dp"), lax.axis_size("groups")
        me, group = lax.axis_index("dp"), lax.axis_index("groups")
        for index, (step, turn) in enumerate(places):
            place = lax.rem(me + step, ranks) * (piece_rows * groups)
            if step:
                place = place + lax.rem(group + turn, groups) * piece_rows
            target = pl.ds(pl.multiple_of(place, 16), pieces[index].shape[0])
            copies.append(
                pltpu.make_async_copy(pieces[index], point_ref.at[target], sems.at[index])
            )
            copies[-1].start()
    out_ref[...] = middle_of(own_ref, gain_ref, parts, low, size)
    for copy in copies:
        copy.wait()


def final_kernel(low, size, mine_ref, other_ref, res_ref, point_ref, *refs):
    out_ref = refs[-1]
    total = mine_ref[...].astype(jnp.float32) + other_ref[...].astype(jnp.float32)
    branch = jnp.dot(
        total.astype(jnp.bfloat16), point_ref[...], preferred_element_type=jnp.float32
    )
    value = (0.5 * (branch + rows_of(res_ref, low, size))).astype(jnp.bfloat16)
    out_ref[...] = value.reshape(out_ref.shape)


def cost(kind, share=1.0):
    return pl.CostEstimate(
        flops=int(1e9 * FLOPS[kind] * share), bytes_accessed=2**20, transcendentals=0
    )


def per_device(tokens, stem_table, conv_weight, gain_in, gain_mid, point_weight):
    row_count = tokens.shape[1]
    tap_total, kinds, width = stem_table.shape
    depth, inner = conv_weight.shape[1:]
    count, groups = lax.axis_size("dp"), lax.axis_size("groups")
    me, group, strand = (lax.axis_index(axis) for axis in ("dp", "groups", "strand"))
    half = width // 2
    vmem = pl.BlockSpec(memory_space=pltpu.VMEM)
    anywhere = pl.BlockSpec(memory_space=pl.ANY)
    bf16, f32 = jnp.bfloat16, jnp.float32
    params = pltpu.CompilerParams(vmem_limit_bytes=24 * MIB)

    members = count * lax.axis_size("seq")
    bases = lax.all_to_all(
        jnp.broadcast_to(tokens, (members, row_count)), ("dp", "seq"), 0, 0, tiled=True
    )

    table_rows = 16 * kinds
    flat = jnp.pad(
        stem_table.reshape(tap_total * kinds, width), ((0, table_rows - tap_total * kinds), (0, 0))
    )
    table = lax.dynamic_slice_in_dim(
        jnp.concatenate([flat, flat], axis=1), me * depth, width, axis=1
    )
    plain = lax.dynamic_slice_in_dim(flat, strand * half, half, axis=1)
    gain_here = lax.dynamic_slice_in_dim(gain_in, me * depth, depth)[None]

    columns = lax.dynamic_slice_in_dim(point_weight, strand * half, half, axis=1)
    piece_rows = point_weight.shape[0] // groups
    piece = lax.dynamic_slice_in_dim(columns, group * piece_rows, piece_rows, axis=0)
    crossed = [lax.ppermute(piece, "dp", ring_pairs("dp", -step)) for step in range(1, count)]

    weight = conv_weight
    received = [[] for _ in CHUNKS]
    for step in range(1, count):
        for index, (low, size) in enumerate(CHUNKS):
            first, passing = index == 0, index == 1
            rows = row_count // DILATION * size
            outs = [jax.ShapeDtypeStruct((rows, inner), bf16)]
            operands = [bases, table, gain_here, weight]
            scratch = [pltpu.VMEM((rows + 2 * size, depth), bf16)]
            if first:
                outs.append(jax.ShapeDtypeStruct(conv_weight.shape, bf16))
                scratch.append(pltpu.SemaphoreType.DMA)
                operands[3] = pltpu.with_memory_space_constraint(conv_weight, pltpu.HBM)
            if passing:
                outs.append(jax.ShapeDtypeStruct(piece.shape, bf16))
                operands.append(crossed[step - 1])
            elif index:
                operands.append(part)
            result = pl.pallas_call(
                functools.partial(chunk_kernel, step, low, size, row_count, first, len(operands)),
                out_shape=outs,
                in_specs=[vmem] * 3
                + [pl.BlockSpec(memory_space=pltpu.HBM) if first else vmem]
                + [anywhere] * (len(operands) - 4),
                out_specs=[vmem, anywhere if passing else vmem][: len(outs)],
                scratch_shapes=scratch,
                input_output_aliases={4: 1} if passing else {},
                compiler_params=params,
                cost_estimate=cost('sent' if index else 'early', size / 64),
                name="conv_sent",
            )(*operands)
            part = result[0]
            if first:
                weight = result[1]
            if passing:
                crossed[step - 1] = result[1]
            received[index].append(lax.ppermute(part, "dp", ring_pairs("dp", step)))

    first_rows = row_count // DILATION * CHUNKS[0][1]
    own, res, middle = pl.pallas_call(
        functools.partial(own_kernel, CHUNKS[0]),
        out_shape=[
            jax.ShapeDtypeStruct((row_count, inner), f32),
            jax.ShapeDtypeStruct((row_count, half), f32),
            jax.ShapeDtypeStruct((first_rows, inner), bf16),
        ],
        in_specs=[vmem] * (5 + count),
        out_specs=[vmem] * 3,
        scratch_shapes=[pltpu.VMEM((row_count + 2 * DILATION, depth), bf16)],
        compiler_params=params,
        cost_estimate=cost('own'),
        name="conv_own",
    )(bases, table, plain, gain_here, weight, gain_mid[None], *received[0])

    places, pieces = [(0, 0)], [columns]
    for step in range(1, count):
        for turn in range(groups):
            part = crossed[step - 1]
            if turn:
                part = lax.ppermute(part, "groups", ring_pairs("groups", -turn))
            places.append((step, turn))
            pieces.append(part)

    middles = [middle]
    for index, (low, size) in list(enumerate(CHUNKS))[1:]:
        rows = row_count // DILATION * size
        taken = middles[1:] if index > 1 else pieces
        result = pl.pallas_call(
            functools.partial(
                middle_kernel, low, size, count - 1, [] if index > 1 else places, piece_rows
            ),
            out_shape=[jax.ShapeDtypeStruct((rows, inner), bf16)]
            + [jax.ShapeDtypeStruct((inner, half), bf16)] * (index == 1),
            in_specs=[vmem] * (count + 1) + [anywhere] * len(taken),
            out_specs=[vmem] * (1 + (index == 1)),
            scratch_shapes=[pltpu.SemaphoreType.DMA((len(taken),))] if index == 1 else [],
            compiler_params=params,
            cost_estimate=cost('middle', size / 64),
            name="middle",
        )(own, gain_mid[None], *received[index], *taken)
        if index == 1:
            point = result[1]
        middles.append(result[0])

    out = None
    for middle, (low, size) in zip(middles, CHUNKS):
        other = lax.ppermute(middle, "strand", ring_pairs("strand", 1))
        operands = [middle, other, res, point] + ([] if out is None else [out])
        out = pl.pallas_call(
            functools.partial(final_kernel, low, size),
            grid=(1,),
            out_shape=jax.ShapeDtypeStruct((row_count // DILATION, DILATION, half), bf16),
            in_specs=[vmem] * 4 + [anywhere] * (len(operands) - 4),
            out_specs=pl.BlockSpec(
                (row_count // DILATION, size, half), lambda i, at=low // size: (0, at, 0)
            ),
            input_output_aliases={} if out is None else {4: 0},
            compiler_params=params,
            cost_estimate=cost('final', size / 64),
            name="final",
        )(*operands)
    return out.reshape(1, row_count, half)


def solution(mesh):
    return jax.shard_map(
        per_device,
        mesh=mesh,
        in_specs=(P(("groups", "dp"), "seq"), P(), P(None, "dp", None), P(), P(), P("dp", None)),
        out_specs=P(("groups", "dp"), "seq", "strand"),
        check_vma=False,
    )
```

time: 41.9 us -> 40.5 us (0.967)
  waiting for transfers between devices: 11.9 us -> 7.43 us
  Pallas kernels: 12.5 us -> 14.9 us
  starting transfers between devices: 13.1 us -> 13.9 us
  other arithmetic: 0.78 us -> 0.11 us
  local copies, waits for them, and re-layouts: 3.09 us -> 3.63 us
    all_to_all x0 -> x1, starting transfers between devices: none -> 7.25 us  [per_device(): lax.all_to_all(jnp.broadcast_to(tokens, (members, row_count)), ('dp', 'se...]
    ppermute x7 -> x5, starting transfers between devices: 12.9 us -> 6.39 us  [the longest x3 2.78 us: per_device(): received[index].append(lax.ppermute(part, 'dp', ring_pairs('dp', step)))]
    ppermute x7 -> x5, waiting for transfers between devices: 11.5 us -> 5.21 us  [the longest x3 4.31 us: per_device(): received[index].append(lax.ppermute(part, 'dp', ring_pairs('dp', step)))]
    pallas_call x7 -> x9, Pallas kernels: 12.5 us -> 14.9 us  [the longest x3 6.6 us: per_device(): pl.pallas_call(functools.partial(chunk_kernel, step, low, size, row_count...]
    all_to_all x0 -> x1, waiting for transfers between devices: none -> 2.21 us  [per_device(): lax.all_to_all(jnp.broadcast_to(tokens, (members, row_count)), ('dp', 'se...]
    broadcast_in_dim x1, local copies, waits for them, and re-layouts: 0.01 us -> 1.32 us  [per_device(): jnp.broadcast_to(tokens, (members, row_count))]
    slice x1 -> x0, local copies, waits for them, and re-layouts: 0.77 us -> none  [per_device(): base_ids[row_count - REACH:]]
    concatenate x1 -> x0, other arithmetic: 0.69 us -> none  [per_device(): near = jnp.concatenate([low, base_ids, high])[None]]
  transfers between devices with their start and end apart: 9 -> 9, of which waited for: 5 -> 4; matrix products, arithmetic and copies ran while one was open for 7% -> 6% of each run, Pallas kernels for 27% -> 35%
where the time goes in v3:
time: 40.5 us; the launch traced here: 40.1 us
  Pallas kernels  14.9 us (37%)
  starting transfers between devices  13.9 us (34%)
  waiting for transfers between devices  7.43 us (18%)
  local copies, waits for them, and re-layouts  3.63 us (9%)
    all_to_all x1, starting transfers between devices, per_device(): lax.all_to_all(jnp.broadcast_to(tokens, (members, row_count)), ('dp', 'se...  7.25 us
    pallas_call x3, Pallas kernels, per_device(): pl.pallas_call(functools.partial(chunk_kernel, step, low, size, row_count...  6.6 us
    ppermute x3, waiting for transfers between devices, per_device(): received[index].append(lax.ppermute(part, 'dp', ring_pairs('dp', step)))  4.31 us
    pallas_call x1, Pallas kernels, per_device(): pl.pallas_call(functools.partial(own_kernel, CHUNKS[0]), out_shape=[jax.S...  4.14 us
    pallas_call x3, Pallas kernels, per_device(): pl.pallas_call(functools.partial(final_kernel, low, size), grid=(1,), out...  3.26 us
    ppermute x3, starting transfers between devices, per_device(): received[index].append(lax.ppermute(part, 'dp', ring_pairs('dp', step)))  2.78 us
    all_to_all x1, waiting for transfers between devices, per_device(): lax.all_to_all(jnp.broadcast_to(tokens, (members, row_count)), ('dp', 'se...  2.21 us
    ppermute x1, starting transfers between devices, per_device(): lax.ppermute(piece, 'dp', ring_pairs('dp', -step))  2.09 us
  transfers between devices with their start and end apart: 9, of which 4 were waited for; matrix products, arithmetic and copies ran while one was open for 6% of the time, Pallas kernels for 35%

profile of v3, /device:TPU:0, one launch (start us, length us, event | category | flops | bytes accessed | tf_op | source)
XLA Modules:
  0.0 40.1 jit_solution(4946991644962627092)
XLA Ops:
  0.0 1.3 %broadcast_in_dim.6 = s32[8,1,512]{2,1,0:T(1,128)} broadcast(s32[512]{0:T(512)} %bitcast.9), dimensions={2} | broadcast | bytes 18432 | tf_op jit(solution)/shard_map/broadcast_in_dim | solution.py:182
  1.3 7.3 %all-to-all-start = ((s32[8,1,512]{2,1,0:T(1,128)}), s32[8,1,512]{2,1,0:T(1,128)S(1)}, u32[]{:S(2)}, u32[]{:S(2)}) async-start(s32[8,1,512]{2,1,0:T(1,128)} %broadcast_in_dim.6), calls=%async_computation | async-start | bytes 32768 | tf_op jit(solution)/shard_map/all_to_all | solution.py:181
  8.6 1.2 %dynamic_slice.18 = bf16[192,768]{1,0:T(8,128)(2,1)S(1)} dynamic-slice(bf16[384,1536]{1,0:T(8,128)(2,1)} %param.11, s32[]{:T(128)S(6)} %select_n.21, s32[]{:T(128)S(6)} %select_n.22), dynamic_slice_sizes={192,768} | dynamic-slice | bytes 589828 | tf_op jit(solution)/shard_map/dynamic_slice | solution.py:197
  9.7 2.1 %collective-permute-start.1 = (bf16[192,768]{1,0:T(8,128)(2,1)S(1)}, bf16[192,768]{1,0:T(8,128)(2,1)S(1)}, u32[]{:S(2)}, u32[]{:S(2)}) collective-permute-start(bf16[192,768]{1,0:T(8,128)(2,1)S(1)} %dynamic_slice.18), channel_id=1, source_target_pairs={{0,2},{2,0},{1,3},{3,1},{4,6},{6,4},{5,7},{7,5},{8,10},{10,8},{9,1... | collective-permute-start | bytes 884744 | tf_op jit(solution)/shard_map/ppermute | solution.py:198
  11.8 1.0 %reshape.12 = bf16[60,1536]{1,0:T(8,128)(2,1)S(1)} reshape(bf16[15,4,1536]{2,1,0:T(4,128)(2,1)} %param.7) | data formatting | bytes 368640 | tf_op jit(solution)/shard_map/reshape | solution.py:187
  12.8 0.1 fusion.refs_1_
  13.0 0.1 dynamic_slice.17
  13.1 2.2 %all-to-all-done = s32[8,1,512]{2,1,0:T(1,128)S(1)} async-done(((s32[8,1,512]{2,1,0:T(1,128)}), s32[8,1,512]{2,1,0:T(1,128)S(1)}, u32[]{:S(2)}, u32[]{:S(2)}) %all-to-all-start) | async-done | bytes 16416 | tf_op jit(solution)/shard_map/all_to_all | solution.py:181
  15.3 2.8 %conv_sent.3 = (bf16[128,768]{1,0:T(8,128)(2,1)S(1)}, bf16[3,768,768]{2,1,0:T(8,128)(2,1)S(1)}) custom-call(s32[8,512]{1,0:T(8,128)S(1)} %bitcast.5, bf16[64,1536]{1,0:T(8,128)(2,1)S(1)} %fusion.refs_1_, f32[1,768]{1,0:T(1,128)S(1)} %broadcast_in_dim.14.refs_2_.refs_3_, bf16[3,768,768]{2,1,0:T(8,128)(2,1)} %refs_3_.1), custom_call_target="tpu_custom_call" | custom-call | flops 100000000 | bytes 1048576 | tf_op jit(solution)/shard_map/conv_sent/pallas_call | solution.py:218
  18.1 0.6 %collective-permute-start = (bf16[128,768]{1,0:T(8,128)(2,1)S(1)}, bf16[128,768]{1,0:T(8,128)(2,1)S(1)}, u32[]{:S(2)}, u32[]{:S(2)}) collective-permute-start(bf16[128,768]{1,0:T(8,128)(2,1)S(1)} %get-tuple-element.15), channel_id=1, source_target_pairs={{0,2},{2,0},{1,3},{3,1},{4,6},{6,4},{5,7},{7,5},{8,10},{10,8},{9,1... | collective-permute-start | bytes 589832 | tf_op jit(solution)/shard_map/ppermute | solution.py:236
  18.8 2.1 %conv_sent.4 = (bf16[256,768]{1,0:T(8,128)(2,1)S(1)}, bf16[192,768]{1,0:T(8,128)(2,1)S(1)}) custom-call(s32[8,512]{1,0:T(8,128)S(1)} %bitcast.6, bf16[64,1536]{1,0:T(8,128)(2,1)S(1)} %fusion.refs_1_, f32[1,768]{1,0:T(1,128)S(1)} %broadcast_in_dim.14.refs_2_.refs_3_, ...), custom_call_target="tpu_custom_call", output_to_operand_aliasing={{1}: (4, {})} | custom-call | flops 2000000000 | bytes 1048576 | tf_op jit(solution)/shard_map/conv_sent/pallas_call | solution.py:218
  20.9 1.8 %collective-permute-start.3 = (bf16[256,768]{1,0:T(8,128)(2,1)S(1)}, bf16[256,768]{1,0:T(8,128)(2,1)S(1)}, u32[]{:S(2)}, u32[]{:S(2)}) collective-permute-start(bf16[256,768]{1,0:T(8,128)(2,1)S(1)} %get-tuple-element.17.refs_4_), channel_id=1, source_target_pairs={{0,2},{2,0},{1,3},{3,1},{4,6},{6,4},{5,7},{7,5},{8,10},{10,8},{9,1... | collective-permute-start | bytes 1179656 | tf_op jit(solution)/shard_map/ppermute | solution.py:236
  22.6 1.7 %conv_sent.5 = bf16[128,768]{1,0:T(8,128)(2,1)S(1)} custom-call(s32[8,512]{1,0:T(8,128)S(1)} %bitcast.7, bf16[64,1536]{1,0:T(8,128)(2,1)S(1)} %fusion.refs_1_, f32[1,768]{1,0:T(1,128)S(1)} %broadcast_in_dim.14.refs_2_.refs_3_, bf16[3,768,768]{2,1,0:T(8,128)(2,1)S(1)} %get-tuple-element.14.refs_4_.refs_3_, bf16[256,768]{1,0:T(8,128)(2,1)S(1)} %get-tuple-element.17.refs_4_), custom_call_target="tpu_custom_call" | custom-call | flops 1000000000 | bytes 1048576 | tf_op jit(solution)/shard_map/conv_sent/pallas_call | solution.py:218
  24.3 0.4 collective-permute-start.2
  24.7 1.5 %collective-permute-start.4 = (bf16[192,768]{1,0:T(8,128)(2,1)S(1)}, bf16[192,768]{1,0:T(8,128)(2,1)S(1)}, u32[]{:S(2)}, u32[]{:S(2)}) collective-permute-start(bf16[192,768]{1,0:T(8,128)(2,1)S(1)} %get-tuple-element.18.refs_2_), channel_id=1, source_target_pairs={{0,16},{16,0},{1,17},{17,1},{2,18},{18,2},{3,19},{19,3},{4,20},{20... | collective-permute-start | bytes 884744 | tf_op jit(solution)/shard_map/ppermute | solution.py:259
  26.2 4.1 %conv_own.1 = (f32[512,768]{1,0:T(8,128)S(1)}, f32[512,768]{1,0:T(8,128)S(1)}, bf16[128,768]{1,0:T(8,128)(2,1)S(1)}) custom-call(s32[8,512]{1,0:T(8,128)S(1)} %bitcast.8, bf16[64,1536]{1,0:T(8,128)(2,1)S(1)} %fusion.refs_1_, bf16[64,768]{1,0:T(8,128)(2,1)S(1)} %constant_dynamic-slice_fusion.1.refs_2_, f32[1,768]{1,0:T(1,128)S(1)} %broadcast_in_dim.14.refs_2_.refs_3_, ...), custom_call_target="tpu_custom_call" | custom-call | flops 10000000000 | bytes 1048576 | tf_op jit(solution)/shard_map/conv_own/pallas_call | solution.py:239
  30.5 0.9 %collective-permute-done.4.refs_3_ = bf16[192,768]{1,0:T(8,128)(2,1)S(1)} collective-permute-done((bf16[192,768]{1,0:T(8,128)(2,1)S(1)}, bf16[192,768]{1,0:T(8,128)(2,1)S(1)}, u32[]{:S(2)}, u32[]{:S(2)}) %collective-permute-start.4) | collective-permute-done | bytes 294944 | tf_op jit(solution)/shard_map/ppermute | solution.py:259
  31.4 2.9 %collective-permute-done.3.refs_0_ = bf16[256,768]{1,0:T(8,128)(2,1)S(1)} collective-permute-done((bf16[256,768]{1,0:T(8,128)(2,1)S(1)}, bf16[256,768]{1,0:T(8,128)(2,1)S(1)}, u32[]{:S(2)}, u32[]{:S(2)}) %collective-permute-start.3) | collective-permute-done | bytes 393248 | tf_op jit(solution)/shard_map/ppermute | solution.py:236
  34.3 0.7 %middle.2 = (bf16[256,768]{1,0:T(8,128)(2,1)S(1)}, bf16[768,768]{1,0:T(8,128)(2,1)S(1)}) custom-call(f32[512,768]{1,0:T(8,128)S(1)} %get-tuple-element.16.own_ref, f32[1,768]{1,0:T(1,128)S(1)} %broadcast_in_dim.15.refs_5_.gain_ref, bf16[256,768]{1,0:T(8,128)(2,1)S(1)} %collective-permute-done.3.refs_0_, ...), custom_call_target="tpu_custom_call" | custom-call | flops 600000000 | bytes 1048576 | tf_op jit(solution)/shard_map/middle/pallas_call | solution.py:267
  35.1 1.4 %collective-permute-done.2.refs_0_ = bf16[128,768]{1,0:T(8,128)(2,1)S(1)} collective-permute-done((bf16[128,768]{1,0:T(8,128)(2,1)S(1)}, bf16[128,768]{1,0:T(8,128)(2,1)S(1)}, u32[]{:S(2)}, u32[]{:S(2)}) %collective-permute-start.2) | collective-permute-done | bytes 196640 | tf_op jit(solution)/shard_map/ppermute | solution.py:236
  36.5 0.2 middle.3.mine_ref
  36.8 1.0 %final.3.refs_0_ = bf16[2,256,768]{2,1,0:T(8,128)(2,1)} custom-call(bf16[128,768]{1,0:T(8,128)(2,1)S(1)} %get-tuple-element.22.mine_ref, bf16[128,768]{1,0:T(8,128)(2,1)S(1)} %collective-permute-done.7.other_ref, f32[512,768]{1,0:T(8,128)S(1)} %get-tuple-element.20.res_ref, bf16[768,768]{1,0:T(8,128)(2,1)S(1)} %get-tuple-element.21.point_ref), custom_call_target="tpu_custom_call" | custom-call | flops 10000000000 | bytes 1048576 | tf_op jit(solution)/shard_map/final/pallas_call | solution.py:288
  37.9 1.2 %final.4.refs_0_ = bf16[2,256,768]{2,1,0:T(8,128)(2,1)} custom-call(bf16[256,768]{1,0:T(8,128)(2,1)S(1)} %get-tuple-element.19.refs_1_.mine_ref, bf16[256,768]{1,0:T(8,128)(2,1)S(1)} %collective-permute-done.6.other_ref, f32[512,768]{1,0:T(8,128)S(1)} %get-tuple-element.20.res_ref, ...), custom_call_target="tpu_custom_call", output_to_operand_aliasing={{}: (4, {})} | custom-call | flops 20000000000 | bytes 1048576 | tf_op jit(solution)/shard_map/final/pallas_call | solution.py:288
  39.1 1.0 %final.5 = bf16[2,256,768]{2,1,0:T(8,128)(2,1)} custom-call(bf16[128,768]{1,0:T(8,128)(2,1)S(1)} %middle.3.mine_ref, bf16[128,768]{1,0:T(8,128)(2,1)S(1)} %collective-permute-done.5.other_ref, f32[512,768]{1,0:T(8,128)S(1)} %get-tuple-element.20.res_ref, bf16[768,768]{1,0:T(8,128)(2,1)S(1)} %get-tuple-element.21.point_ref, ...), custom_call_target="tpu_custom_call", output_to_operand_aliasing={{}: (4, {})} | custom-call | flops 10000000000 | bytes 1048576 | tf_op jit(solution)/shard_map/final/pallas_call | solution.py:288
  (20 shorter events, 0.3 us)
Async XLA Ops:
  0.0 13.0 %copy-start.2 = (f32[1536]{0:T(1024)S(1)}, f32[1536]{0:T(1024)}, u32[]{:S(2)}) copy-start(f32[1536]{0:T(1024)} %param.9) | copy-start | bytes 18436
  0.0 13.1 %copy-start.1 = (f32[768]{0:T(1024)S(1)}, f32[768]{0:T(1024)}, u32[]{:S(2)}) copy-start(f32[768]{0:T(1024)} %param.10) | copy-start | bytes 9220
  1.3 14.0 %all-to-all-start = ((s32[8,1,512]{2,1,0:T(1,128)}), s32[8,1,512]{2,1,0:T(1,128)S(1)}, u32[]{:S(2)}, u32[]{:S(2)}) async-start(s32[8,1,512]{2,1,0:T(1,128)} %broadcast_in_dim.6), calls=%async_computation | async-start | bytes 32768 | tf_op jit(solution)/shard_map/all_to_all | solution.py:181
  9.7 9.0 %collective-permute-start.1 = (bf16[192,768]{1,0:T(8,128)(2,1)S(1)}, bf16[192,768]{1,0:T(8,128)(2,1)S(1)}, u32[]{:S(2)}, u32[]{:S(2)}) collective-permute-start(bf16[192,768]{1,0:T(8,128)(2,1)S(1)} %dynamic_slice.18), channel_id=1, source_target_pairs={{0,2},{2,0},{1,3},{3,1},{4,6},{6,4},{5,7},{7,5},{8,10},{10,8},{9,1... | collective-permute-start | bytes 884744 | tf_op jit(solution)/shard_map/ppermute | solution.py:198
  18.1 8.1 %collective-permute-start = (bf16[128,768]{1,0:T(8,128)(2,1)S(1)}, bf16[128,768]{1,0:T(8,128)(2,1)S(1)}, u32[]{:S(2)}, u32[]{:S(2)}) collective-permute-start(bf16[128,768]{1,0:T(8,128)(2,1)S(1)} %get-tuple-element.15), channel_id=1, source_target_pairs={{0,2},{2,0},{1,3},{3,1},{4,6},{6,4},{5,7},{7,5},{8,10},{10,8},{9,1... | collective-permute-start | bytes 589832 | tf_op jit(solution)/shard_map/ppermute | solution.py:236
  20.9 13.4 %collective-permute-start.3 = (bf16[256,768]{1,0:T(8,128)(2,1)S(1)}, bf16[256,768]{1,0:T(8,128)(2,1)S(1)}, u32[]{:S(2)}, u32[]{:S(2)}) collective-permute-start(bf16[256,768]{1,0:T(8,128)(2,1)S(1)} %get-tuple-element.17.refs_4_), channel_id=1, source_target_pairs={{0,2},{2,0},{1,3},{3,1},{4,6},{6,4},{5,7},{7,5},{8,10},{10,8},{9,1... | collective-permute-start | bytes 1179656 | tf_op jit(solution)/shard_map/ppermute | solution.py:236
  24.3 12.2 %collective-permute-start.2 = (bf16[128,768]{1,0:T(8,128)(2,1)S(1)}, bf16[128,768]{1,0:T(8,128)(2,1)S(1)}, u32[]{:S(2)}, u32[]{:S(2)}) collective-permute-start(bf16[128,768]{1,0:T(8,128)(2,1)S(1)} %conv_sent.5), channel_id=1, source_target_pairs={{0,2},{2,0},{1,3},{3,1},{4,6},{6,4},{5,7},{7,5},{8,10},{10,8},{9,1... | collective-permute-start | bytes 589832 | tf_op jit(solution)/shard_map/ppermute | solution.py:236
  24.7 5.8 %copy-start = (bf16[384,1536]{1,0:T(8,128)(2,1)S(1)}, bf16[384,1536]{1,0:T(8,128)(2,1)}, u32[]{:S(2)}) copy-start(bf16[384,1536]{1,0:T(8,128)(2,1)} %param.11) | copy-start | bytes 3538948
  24.7 6.7 %collective-permute-start.4 = (bf16[192,768]{1,0:T(8,128)(2,1)S(1)}, bf16[192,768]{1,0:T(8,128)(2,1)S(1)}, u32[]{:S(2)}, u32[]{:S(2)}) collective-permute-start(bf16[192,768]{1,0:T(8,128)(2,1)S(1)} %get-tuple-element.18.refs_2_), channel_id=1, source_target_pairs={{0,16},{16,0},{1,17},{17,1},{2,18},{18,2},{3,19},{19,3},{4,20},{20... | collective-permute-start | bytes 884744 | tf_op jit(solution)/shard_map/ppermute | solution.py:259
  30.4 6.5 %collective-permute-start.7 = (bf16[128,768]{1,0:T(8,128)(2,1)S(1)}, bf16[128,768]{1,0:T(8,128)(2,1)S(1)}, u32[]{:S(2)}, u32[]{:S(2)}) collective-permute-start(bf16[128,768]{1,0:T(8,128)(2,1)S(1)} %get-tuple-element.22.mine_ref), channel_id=1, source_target_pairs={{0,1},{1,0},{2,3},{3,2},{4,5},{5,4},{6,7},{7,6},{8,9},{9,8},{10,11... | collective-permute-start | bytes 589832 | tf_op jit(solution)/shard_map/ppermute | solution.py:286
  35.0 2.8 %collective-permute-start.6 = (bf16[256,768]{1,0:T(8,128)(2,1)S(1)}, bf16[256,768]{1,0:T(8,128)(2,1)S(1)}, u32[]{:S(2)}, u32[]{:S(2)}) collective-permute-start(bf16[256,768]{1,0:T(8,128)(2,1)S(1)} %get-tuple-element.19.refs_1_.mine_ref), channel_id=1, source_target_pairs={{0,1},{1,0},{2,3},{3,2},{4,5},{5,4},{6,7},{7,6},{8,9},{9,8},{10,11... | collective-permute-start | bytes 1179656 | tf_op jit(solution)/shard_map/ppermute | solution.py:286
  36.7 2.3 %collective-permute-start.5 = (bf16[128,768]{1,0:T(8,128)(2,1)S(1)}, bf16[128,768]{1,0:T(8,128)(2,1)S(1)}, u32[]{:S(2)}, u32[]{:S(2)}) collective-permute-start(bf16[128,768]{1,0:T(8,128)(2,1)S(1)} %middle.3.mine_ref), channel_id=1, source_target_pairs={{0,1},{1,0},{2,3},{3,2},{4,5},{5,4},{6,7},{7,6},{8,9},{9,8},{10,11... | collective-permute-start | bytes 589832 | tf_op jit(solution)/shard_map/ppermute | solution.py:286
